TPU v7x, 128 devices: a whole 4x4x4 slice. The times are simulated.
128 devices in a mesh: layer: 8 (over z_lo, y), latent: 16 (over x, z_hi, core).
Axes of the slice: x: 4, y: 4, z: 4 (z_hi: 2, z_lo: 2; z = z_hi * 2 + z_lo), core: 2. Of those that a mesh axis runs over, the one named last changes fastest.
Arguments:
- acts: bfloat16 [1024, 8, 2048], P('latent', 'layer'), may hold values from -6 to 6
- enc_weight: bfloat16 [8, 2048, 16384], P('layer', None, 'latent'), may hold values from -0.046875 to 0.046875
- enc_bias: float32 [16384], P('latent'), may hold values from -1 to 0.5
- dec_weight: bfloat16 [16384, 8, 2048], P('latent', 'layer'), may hold values from -2 to 2
- dec_bias: float32 [8, 2048], P('layer'), may hold values from -3 to 3
Outputs:
- enc_grad: float32 [8, 2048, 16384], P('layer', None, 'latent')
- enc_bias_grad: float32 [16384], P('latent')
- dec_grad: float32 [16384, 8, 2048], P('latent', 'layer')
- dec_bias_grad: float32 [8, 2048], P('layer')
All inputs are finite; a program needn't handle non-finite values.
Results may differ from a plain program's by a relative error of at most 0.0041.
Values may be sent and summed in bfloat16 or wider, within the bound.
A program may use at most 128 MiB of HBM per device.

v0:
```python
import math

import jax
import jax.numpy as jnp
from jax import lax
from jax.sharding import PartitionSpec as P

PENALTY = 0.05
EPS = 1e-06


def contract_rows(left, right):
    return lax.dot_general(
        left, right, (((0,), (0,)), ((), ())), preferred_element_type=jnp.float32
    )


def on_device(acts, enc_weight, enc_bias, dec_weight, dec_bias):
    tok_dev, layers_dev, width = acts.shape
    lanes = layers_dev * width
    latents_dev = enc_weight.shape[2]
    tokens = tok_dev * lax.axis_size("latent")
    scale = 1.0 / math.sqrt(tokens)
    enc_flat = enc_weight.reshape(lanes, latents_dev)
    dec_flat = dec_weight.reshape(latents_dev, lanes)
    own_rows = acts.reshape(tok_dev, lanes)
    gathered = lax.all_gather(own_rows, "latent", axis=0, tiled=True)
    norms = jnp.sqrt(jnp.sum(jnp.square(dec_weight.astype(jnp.float32)), axis=2) + EPS)
    norm_part = jnp.sum(norms, axis=1)
    pre_part = jnp.dot(gathered, enc_flat, preferred_element_type=jnp.float32)
    pre_sum, totals = lax.psum((pre_part, norm_part), "layer")
    pre = pre_sum + enc_bias
    active = jnp.maximum(pre, 0.0)
    codes = (active * active).astype(jnp.bfloat16)
    rows = codes
    recon = (
        lax.psum_scatter(
            jnp.dot(rows, dec_flat, preferred_element_type=jnp.float32),
            "latent",
            scatter_dimension=0,
            tiled=True,
        )
        + dec_bias
    )
    recon_grad = (recon - own_rows.astype(jnp.float32)) * scale
    dec_bias_grad = lax.psum(jnp.sum(recon_grad, axis=0), "latent").reshape(layers_dev, width)
    recon_low = recon_grad.astype(jnp.bfloat16)
    piece = lax.all_gather(recon_low, "latent", axis=0, tiled=True)
    rows = codes
    dec_total = contract_rows(rows, piece)
    block = lax.dot_general(
        piece, dec_flat, (((1,), (1,)), ((), ())), preferred_element_type=jnp.float32
    )
    dec_total, code_part = (dec_total, block)
    code_grad = lax.psum(code_part, "layer") + PENALTY * scale * totals
    pre_grad = code_grad * (2.0 * active)
    enc_bias_grad = jnp.sum(pre_grad, axis=0)
    pre_low = pre_grad.astype(jnp.bfloat16)
    enc_grad = contract_rows(gathered, pre_low).reshape(layers_dev, width, latents_dev)
    code_sums = jnp.sum(codes, axis=0, dtype=jnp.float32)
    dec_grad = dec_total.reshape(latents_dev, layers_dev, width)
    dec_grad = (
        dec_grad
        + PENALTY
        * scale
        * code_sums[:, None, None]
        * dec_weight.astype(jnp.float32)
        / norms[:, :, None]
    )
    return (enc_grad, enc_bias_grad, dec_grad, dec_bias_grad)


def solution(mesh):
    return jax.shard_map(
        on_device,
        mesh=mesh,
        in_specs=(
            P("latent", "layer", None),
            P("layer", None, "latent"),
            P("latent"),
            P("latent", "layer", None),
            P("layer", None),
        ),
        out_specs=(
            P("layer", None, "latent"),
            P("latent"),
            P("latent", "layer", None),
            P("layer", None),
        ),
        check_vma=False,
    )
```

profile of v0, /device:TPU:96, one launch (start us, length us, event | category | flops | bytes accessed | tf_op | source)
XLA Modules:
  0.0 520.6 jit_solution(3719644296865682083)
XLA Ops:
  7.2 0.0 all-gather.6.cloned.1.call-start
  7.2 0.7 all-gather.6.cloned.1.call-update
  7.9 0.0 all-reduce.3.cloned.1.call-start
  7.9 58.0 %all-gather.6.cloned.1.call-done = bf16[1024,1,2048]{2,0,1:T(8,128)(2,1)} async-done(((bf16[64,1,2048]{2,0,1:T(8,128)(2,1)}), bf16[1024,1,2048]{2,0,1:T(8,128)(2,1)}) %all-gather.6.cloned.1.call-update) | async-done | bytes 4194320 | tf_op jit(solution)/shard_map/all_gather | solution.py:27
  65.9 10.0 %fusion.7 = f32[1024,1024]{1,0:T(8,128)} fusion(bf16[1,2048,1024]{2,1,0:T(8,128)(2,1)} %param.6, bf16[1024,1,2048]{2,0,1:T(8,128)(2,1)} %all-gather.6.cloned.1.call-done), kind=kOutput, calls=%fused_computation.10 | convolution fusion | flops 4294967296 | bytes 12582912 | tf_op jit(solution)/shard_map/dot_general | solution.py:30
  75.9 0.0 all-reduce.3.cloned.1.call-update
  75.9 0.0 reduce-scatter.2.cloned.1.call-start
  75.9 105.2 %all-reduce.3.cloned.1.call-done = f32[1024,1024]{1,0:T(8,128)} async-done(((f32[1024,1024]{1,0:T(8,128)}), f32[1024,1024]{1,0:T(8,128)}) %all-reduce.3.cloned.1.call-update) | async-done | bytes 4194320 | tf_op jit(solution)/shard_map/psum | solution.py:31
  181.1 0.0 copy-done.2
  181.1 0.0 copy-start
  181.1 3.1 convert_reduce_fusion
  184.2 0.4 copy-done
  184.5 6.7 %fusion.5 = f32[1024,2048]{1,0:T(8,128)} fusion(bf16[1024,1024]{1,0:T(8,128)(2,1)S(1)} %get-tuple-element.9, bf16[1024,1,2048]{2,0,1:T(8,128)(2,1)S(1)} %copy-done), kind=kOutput, calls=%fused_computation.8 | convolution fusion | flops 4294967296 | bytes 14680064 | tf_op jit(solution)/shard_map/dot_general | solution.py:38
  191.2 0.0 reduce-scatter.2.cloned.1.call-update
  191.3 0.0 all-gather.4.cloned.1.call-start
  191.3 100.5 %reduce-scatter.2.cloned.1.call-done = f32[64,2048]{1,0:T(8,128)} async-done(((f32[1024,2048]{1,0:T(8,128)}), f32[64,2048]{1,0:T(8,128)}) %reduce-scatter.2.cloned.1.call-update) | async-done | bytes 524304 | tf_op jit(solution)/shard_map/reduce_scatter | solution.py:37
  291.8 0.0 copy-done.1
  291.8 0.0 copy-done.3
  291.8 1.8 fusion.14
  293.7 0.0 all-gather.4.cloned.1.call-update
  293.7 0.0 all-reduce.5.cloned.1.call-start
  293.8 55.6 %all-gather.4.cloned.1.call-done = bf16[1024,2048]{1,0:T(8,128)(2,1)} async-done(((bf16[64,2048]{1,0:T(8,128)(2,1)}), bf16[1024,2048]{1,0:T(8,128)(2,1)}) %all-gather.4.cloned.1.call-update) | async-done | bytes 4194320 | tf_op jit(solution)/shard_map/all_gather | solution.py:48
  349.4 10.0 %fusion.3 = f32[1024,1024]{1,0:T(8,128)} fusion(bf16[1024,2048]{1,0:T(8,128)(2,1)} %all-gather.4.cloned.1.call-done, bf16[1024,1,2048]{2,0,1:T(8,128)(2,1)} %param.8), kind=kOutput, calls=%fused_computation.6 | convolution fusion | flops 4294967296 | bytes 12582912 | tf_op jit(solution)/shard_map/dot_general | solution.py:51
  359.4 0.0 all-reduce.5.cloned.1.call-update
  359.4 3.1 fusion
  362.5 18.3 %psum.30 = f32[1024]{0:T(1024)S(1)} all-reduce(f32[1024]{0:T(1024)S(1)} %add_sqrt_fusion), channel_id=1, replica_groups=mesh['layer'=8,'latent'=16] {'layer'}, use_global_device_ids=true, to_apply=%region_4.0 | all-reduce | flops 1024 | bytes 8192 | tf_op jit(solution)/shard_map/psum | solution.py:31
  380.8 85.2 %psum.31 = f32[1,2048]{1,0:T(1,128)} all-reduce(f32[1,2048]{1,0:T(1,128)S(1)} %bitcast.29), channel_id=1, replica_groups=mesh['layer'=8,'latent'=16] {'latent'}, use_global_device_ids=true, to_apply=%region_8.0 | all-reduce | flops 2048 | bytes 16384 | tf_op jit(solution)/shard_map/psum | solution.py:46
  466.0 8.7 %fusion.2 = f32[1024,1,2048]{2,0,1:T(8,128)S(1)} fusion(bf16[1024,1,2048]{2,0,1:T(8,128)(2,1)} %param.8, bf16[1024,1024]{1,0:T(8,128)(2,1)S(1)} %get-tuple-element.9, bf16[1024,2048]{1,0:T(8,128)(2,1)} %all-gather.4.cloned.1.call-done, f32[1024]{0:T(1024)S(1)} %add_sqrt_fusion, f32[1024]{0:T(1024)S(1)} %broadcast_multiply_fusion), kind=kOutput, calls=%fused_computation.4 | convolution fusion | flops 4303355904 | bytes 18882560 | tf_op jit(solution)/shard_map/dot_general | solution.py:13
  474.7 12.5 %copy.10 = f32[1024,1,2048]{2,1,0:T(1,128)} copy(f32[1024,1,2048]{2,0,1:T(8,128)S(1)} %fusion.2) | data formatting | bytes 16777216
  487.2 12.6 %convolution_bitcast_fusion = f32[1,2048,1024]{1,2,0:T(8,128)} fusion(bf16[1024,1,2048]{2,0,1:T(8,128)(2,1)} %all-gather.6.cloned.1.call-done, f32[1024,1024]{1,0:T(8,128)} %all-reduce.5.cloned.1.call-done, f32[1024,1024]{1,0:T(8,128)} %all-reduce.3.cloned.1.call-done, f32[1024]{0:T(1024)S(1)} %broadcast_multiply_fusion.1, f32[1024]{0:T(1024)S(1)} %copy-done.2), kind=kOutput, calls=%fused_computation.5 | convolution fusion | flops 4301258752 | bytes 20979712 | tf_op jit(solution)/shard_map/dot_general | solution.py:13
  499.8 9.2 %copy.9 = f32[1,2048,1024]{2,1,0:T(8,128)} copy(f32[1,2048,1024]{1,2,0:T(8,128)} %convolution_bitcast_fusion) | data formatting | bytes 16777216
  509.1 5.0 fusion.12
  (7 shorter events, 0.0 us)
Async XLA Ops:
  7.2 58.7 %all-gather.6.cloned.1.call-start = ((), (), s32[]{:S(2)}) async-start(), calls=%async_computation.5 | async-start | bytes 4456448 | tf_op jit(solution)/shard_map/all_gather | solution.py:27
  7.9 173.2 %all-reduce.3.cloned.1.call-start = ((), (), s32[]{:S(2)}) async-start(), calls=%async_computation.1 | async-start | bytes 8388608 | tf_op jit(solution)/shard_map/psum | solution.py:31
  75.9 105.2 %copy-start.2 = (f32[1024]{0:T(1024)S(1)}, f32[1024]{0:T(1024)}, u32[]{:S(2)}) copy-start(f32[1024]{0:T(1024)} %param.7) | copy-start | bytes 12292
  75.9 216.0 %reduce-scatter.2.cloned.1.call-start = ((), (), s32[]{:S(2)}) async-start(), calls=%async_computation.2 | async-start | bytes 8912896 | tf_op jit(solution)/shard_map/reduce_scatter | solution.py:37
  181.1 3.4 copy-start
  191.2 100.6 %copy-start.1 = (bf16[64,1,2048]{2,0,1:T(8,128)(2,1)S(1)}, bf16[64,1,2048]{2,0,1:T(8,128)(2,1)}, u32[]{:S(2)}) copy-start(bf16[64,1,2048]{2,0,1:T(8,128)(2,1)} %param.5) | copy-start | bytes 786436
  191.2 100.6 %copy-start.3 = (f32[1,2048]{1,0:T(1,128)S(1)}, f32[1,2048]{1,0:T(1,128)}, u32[]{:S(2)}) copy-start(f32[1,2048]{1,0:T(1,128)} %param.9) | copy-start | bytes 24580
  191.3 158.1 %all-gather.4.cloned.1.call-start = ((), (), s32[]{:S(2)}) async-start(), calls=%async_computation.3 | async-start | bytes 4456448 | tf_op jit(solution)/shard_map/all_gather | solution.py:48
  293.7 193.5 %all-reduce.5.cloned.1.call-start = ((), (), s32[]{:S(2)}) async-start(), calls=%async_computation.4 | async-start | bytes 8388608 | tf_op jit(solution)/shard_map/psum | solution.py:55
Sparse Core Ops, SparseCore 0:
  10.4 55.4 all-gather.5
  76.0 105.0 all-reduce.2
  191.4 100.4 reduce-scatter.1
  294.7 54.6 all-gather.3
  359.5 105.6 all-reduce.4
where the time goes:
time: 521 us
  waiting for transfers between devices  320 us (61%)
  blocking collectives  104 us (20%)
  matrix products  47.9 us (9%)
  local copies, waits for them, and re-layouts  22.1 us (4%)
  between operations  13.8 us (3%)
  other arithmetic  13 us (2%)
    psum x1, waiting for transfers between devices, on_device(): pre_sum, totals = lax.psum((pre_part, norm_part), 'layer')  105 us
    reduce_scatter x1, waiting for transfers between devices, on_device(): lax.psum_scatter(jnp.dot(rows, dec_flat, preferred_element_type=jnp.float...  101 us
    psum x1, blocking collectives, on_device(): lax.psum(jnp.sum(recon_grad, axis=0), 'latent').reshape(layers_dev, width)  85.2 us
    all_gather x1, waiting for transfers between devices, on_device(): gathered = lax.all_gather(own_rows, 'latent', axis=0, tiled=True)  58 us
    all_gather x1, waiting for transfers between devices, on_device(): piece = lax.all_gather(recon_low, 'latent', axis=0, tiled=True)  55.6 us
    unnamed x10, local copies, waits for them, and re-layouts  22.1 us
    dot_general x2, matrix products, contract_rows(): lax.dot_general(left, right, (((0,), (0,)), ((), ())), preferred_element_...  21.3 us
    psum x1, blocking collectives, on_device(): pre_sum, totals = lax.psum((pre_part, norm_part), 'layer')  18.3 us
  transfers between devices with their start and end apart: 5, of which 4 were waited for; matrix products, arithmetic and copies ran while one was open for 5% of the time, Pallas kernels for 0%

commit v1 on v0

v1 whole, which is shorter than its diff:
```python
import functools
import math

import jax
import jax.numpy as jnp
from jax import lax
from jax.experimental import pallas as pl
from jax.experimental.pallas import tpu as pltpu
from jax.sharding import PartitionSpec as P

PENALTY = 0.05
EPS = 1e-06
MESH = pl.DeviceIdType.MESH
BF16 = jnp.bfloat16
F32 = jnp.float32

TOKENS = 1024
WIDTH = 2048
LATS = 1024
CHUNKS = 4
ROWS = TOKENS // CHUNKS
OWN = 16
SCALE = 1.0 / math.sqrt(TOKENS)
TILE = 256

STAGES = 18
SPAN = 4


def aligned(value, multiple):
    return pl.multiple_of(value, multiple)


CODE = 2.0**18
FLOOR = 2.0**-120


def pack(value):
    value = value * CODE
    return (value * value * (value * jnp.abs(value))).astype(BF16)


def unpack(coded):
    coded = coded.astype(F32)
    size = lax.rsqrt(lax.rsqrt(jnp.maximum(jnp.abs(coded), FLOOR))) * (1.0 / CODE)
    return jnp.where(coded < 0.0, -size, size)


def plain(value):
    return value.astype(BF16)


def widen(value):
    return value.astype(F32)


def step_kernel(
    acts, enc_hbm, enc_bias, dec_hbm, dec_bias,
    g_out, c_out, r_out, p_out, norm_out,
    enc, dec, gath, codes, low, plow,
    full1, full2, send1, send2, recv1, recv2, zsend1, zrecv1, zsend2, zrecv2, keep1, keep2, active,
    full3, send3, crecv, xsend, xrecv, zsend3, zrecv3, keep3, norm_row,
    ssem, rsem, lsem, osem,
):
    a = lax.axis_index("layer")
    b = lax.axis_index("latent")
    zl, y = a // 4, a % 4
    x, zh, c = b // 4, (b // 2) % 2, b % 2

    def ydev(d):
        return (zl * 4 + (y + d) % 4, b)

    zldev = ((1 - zl) * 4 + y, b)

    def xdev(d):
        return (a, ((x + d) % 4) * 4 + zh * 2 + c)

    zhdev = (a, x * 4 + (1 - zh) * 2 + c)
    cdev = (a, x * 4 + zh * 2 + 1 - c)

    load_enc = pltpu.make_async_copy(enc_hbm, enc, lsem.at[0])
    load_dec = pltpu.make_async_copy(dec_hbm, dec, lsem.at[1])
    load_enc.start()
    load_dec.start()

    barrier = pltpu.get_barrier_semaphore()
    peers = [zldev, zhdev, cdev] + [ydev(d) for d in (1, 2, 3)] + [xdev(d) for d in (1, 2, 3)]
    for peer in peers:
        pl.semaphore_signal(barrier, inc=1, device_id=peer, device_id_type=MESH)
    pl.semaphore_wait(barrier, len(peers))

    def push(stage, k, src, dst, device):
        pltpu.make_async_remote_copy(
            src_ref=src, dst_ref=dst, send_sem=ssem.at[stage, k], recv_sem=rsem.at[stage, k],
            device_id=device, device_id_type=MESH,
        ).start()

    def arrived(stage, k, ref):
        pltpu.make_async_copy(ref, ref, rsem.at[stage, k]).wait()

    def gone(stage, k, ref):
        pltpu.make_async_copy(ref, ref, ssem.at[stage, k]).wait()

    lat_slot = pl.ds(aligned(c * 128 + x * 32 + zh * 16, 16), 16)
    lat_zslot = pl.ds(aligned(c * 128 + x * 32 + (1 - zh) * 16, 16), 16)
    core_half = pl.ds(aligned(c * 128, 128), 128)
    lay_slot = pl.ds(aligned(y * 64 + zl * 32, 32), 32)
    lay_zslot = pl.ds(aligned(y * 64 + (1 - zl) * 32, 32), 32)

    def spread_lat(first, k, buf):
        ref = buf.at[k, lat_slot]
        push(first, k, ref, ref, zhdev)
        for d in (1, 2, 3):
            push(first + 1, k, ref, ref, xdev(d))

    def pass_lat(first, k, buf):
        ref = buf.at[k, lat_zslot]
        arrived(first, k, ref)
        for d in (1, 2, 3):
            push(first + 1, k, ref, ref, xdev(d))

    def pair_lat(first, k, buf):
        arrived(first + 1, k, buf.at[k, pl.ds(0, 96)])
        ref = buf.at[k, core_half]
        push(first + 2, k, ref, ref, cdev)

    def done_lat(first, k, buf):
        arrived(first + 2, k, buf.at[k, pl.ds(0, 128)])

    def spread_lay(first, k, buf):
        ref = buf.at[k, lay_slot]
        push(first, k, ref, ref, zldev)
        for d in (1, 2, 3):
            push(first + 1, k, ref, ref, ydev(d))

    def pass_lay(first, k, buf):
        ref = buf.at[k, lay_zslot]
        arrived(first, k, ref)
        for d in (1, 2, 3):
            push(first + 1, k, ref, ref, ydev(d))

    def done_lay(first, k, buf):
        arrived(first + 1, k, buf.at[k, pl.ds(0, 192)])

    def reduce_y(first, k, send, recv):
        for d in (1, 2, 3):
            rows = pl.ds(aligned(((y + d) % 4) * 64, 64), 64)
            push(first, k, send.at[k, rows], recv.at[k, d - 1], ydev(d))

    def reduce_z(first, k, full, recv, zsend, zrecv, keep, narrow, wide):
        arrived(first, k, recv.at[k])

        def total(half):
            value = full[k % 2, pl.ds(aligned(y * 64 + half * 32, 32), 32), :]
            for d in range(3):
                value = value + wide(recv[k, d, pl.ds(aligned(half * 32, 32), 32), :])
            return value

        zsend[k] = narrow(total(1 - zl))
        push(first + 1, k, zsend.at[k], zrecv.at[k], zldev)
        keep[k % 2] = total(zl)

    def m0(k):
        gath[k, lat_slot, :] = acts[pl.ds(aligned(k * OWN, OWN), OWN), :]
        spread_lat(0, k, gath)

    def m1(k):
        pass_lat(0, k, gath)

    def m2(k):
        pair_lat(0, k, gath)

    def m3(k):
        done_lat(0, k, gath)
        pltpu.make_async_copy(gath.at[k], g_out.at[k], osem.at[0]).start()

        def tile(n, _):
            cols = pl.ds(aligned(n * TILE, TILE), TILE)
            value = jnp.dot(gath[k], enc[:, cols], preferred_element_type=F32)
            full1[k % 2, :, cols] = value
            send1[k, :, cols] = pack(value)
            return 0

        lax.fori_loop(0, LATS // TILE, tile, 0)
        reduce_y(3, k, send1, recv1)

    def m4(k):
        reduce_z(3, k, full1, recv1, zsend1, zrecv1, keep1, pack, unpack)

    def m5(k):
        arrived(4, k, zrecv1.at[k])
        pre = keep1[k % 2] + unpack(zrecv1[k]) + enc_bias[...]
        value = jnp.maximum(pre, 0.0)
        active[k] = value
        codes[k, lay_slot, :] = (value * value).astype(BF16)
        spread_lay(5, k, codes)

    def m6(k):
        pass_lay(5, k, codes)

    def m7(k):
        done_lay(5, k, codes)
        pltpu.make_async_copy(codes.at[k], c_out.at[k], osem.at[1]).start()

        def tile(n, _):
            cols = pl.ds(aligned(n * TILE, TILE), TILE)
            value = jnp.dot(codes[k], dec[:, cols], preferred_element_type=F32)
            full3[k % 2, :, cols] = value
            send3[k, :, cols] = value.astype(BF16)
            return 0

        lax.fori_loop(0, WIDTH // TILE, tile, 0)
        other = pl.ds(aligned((1 - c) * 128, 128), 128)
        push(7, k, send3.at[k, other], crecv.at[k], cdev)

    def m8(k):
        arrived(7, k, crecv.at[k])
        for d in (1, 2, 3):
            to = (x + d) % 4
            value = full3[k % 2, pl.ds(aligned(c * 128 + to * 32, 32), 32), :]
            value = value + crecv[k, pl.ds(aligned(to * 32, 32), 32), :].astype(F32)
            xsend[k, d - 1] = value.astype(BF16)
            push(8, k, xsend.at[k, d - 1], xrecv.at[k, d - 1], xdev(d))

    def m9(k):
        arrived(8, k, xrecv.at[k])

        def total(half):
            value = full3[k % 2, pl.ds(aligned(c * 128 + x * 32 + half * 16, 16), 16), :]
            value = value + crecv[k, pl.ds(aligned(x * 32 + half * 16, 16), 16), :].astype(F32)
            for d in range(3):
                value = value + xrecv[k, d, pl.ds(aligned(half * 16, 16), 16), :].astype(F32)
            return value

        zsend3[k] = total(1 - zh).astype(BF16)
        push(9, k, zsend3.at[k], zrecv3.at[k], zhdev)
        keep3[k % 2] = total(zh)

    def m10(k):
        arrived(9, k, zrecv3.at[k])
        recon = keep3[k % 2] + zrecv3[k].astype(F32) + dec_bias[...]
        flat = acts[pl.ds(aligned(k * OWN, OWN), OWN), :].astype(F32)
        low[k, lat_slot, :] = ((recon - flat) * SCALE).astype(BF16)
        spread_lat(10, k, low)

    def m11(k):
        pass_lat(10, k, low)

    def m12(k):
        pair_lat(10, k, low)

    def m13(k):
        done_lat(10, k, low)
        pltpu.make_async_copy(low.at[k], r_out.at[k], osem.at[2]).start()

        def tile(n, _):
            cols = pl.ds(aligned(n * TILE, TILE), TILE)
            value = lax.dot_general(
                low[k], dec[cols, :], (((1,), (1,)), ((), ())), preferred_element_type=F32
            )
            value = value + (PENALTY * SCALE) * norm_row[0:1, cols]
            full2[k % 2, :, cols] = value
            send2[k, :, cols] = value.astype(BF16)
            return 0

        lax.fori_loop(0, LATS // TILE, tile, 0)
        reduce_y(13, k, send2, recv2)

    def m14(k):
        reduce_z(13, k, full2, recv2, zsend2, zrecv2, keep2, plain, widen)

    def m15(k):
        arrived(14, k, zrecv2.at[k])
        code_grad = keep2[k % 2] + zrecv2[k].astype(F32)
        plow[k, lay_slot, :] = (code_grad * (2.0 * active[k])).astype(BF16)
        spread_lay(15, k, plow)

    def m16(k):
        pass_lay(15, k, plow)

    def m17(k):
        done_lay(15, k, plow)
        pltpu.make_async_copy(plow.at[k], p_out.at[k], osem.at[3]).start()

    def norms():
        def tile(n, _):
            rows = pl.ds(aligned(n * 128, 128), 128)
            value = dec[rows, :].astype(F32)
            norm = jnp.sqrt(jnp.sum(value * value, axis=1, keepdims=True) + EPS)
            wide = jnp.broadcast_to(norm, (128, 128))
            norm_out[rows, :] = wide
            norm_row[:, rows] = wide.T[0:8, :]
            return 0

        lax.fori_loop(0, LATS // 128, tile, 0)

    stages = [m0, m1, m2, m3, m4, m5, m6, m7, m8, m9, m10, m11, m12, m13, m14, m15, m16, m17]

    def iteration(t, _):
        for place in range(SPAN):
            for m in reversed(range(place, STAGES, SPAN)):
                k = t - m // SPAN
                pl.when(jnp.logical_and(k >= 0, k < CHUNKS))(functools.partial(stages[m], k))
            if place == 0:

                @pl.when(t == 0)
                def _():
                    load_enc.wait()
                    load_dec.wait()
                    norms()

        return 0

    lax.fori_loop(0, CHUNKS + (STAGES - 1) // SPAN, iteration, 0)

    def drain(k, _):
        for first, buf in ((0, gath), (10, low)):
            gone(first, k, buf.at[k, pl.ds(0, 16)])
            gone(first + 1, k, buf.at[k, pl.ds(0, 96)])
            gone(first + 2, k, buf.at[k, pl.ds(0, 128)])
        for first, send in ((3, send1), (13, send2)):
            gone(first, k, send.at[k, pl.ds(0, 192)])
            gone(first + 1, k, send.at[k, pl.ds(0, 32)])
        for first, buf in ((5, codes), (15, plow)):
            gone(first, k, buf.at[k, pl.ds(0, 32)])
            gone(first + 1, k, buf.at[k, pl.ds(0, 192)])
        gone(7, k, crecv.at[k])
        gone(8, k, xsend.at[k])
        gone(9, k, zsend3.at[k])
        return 0

    lax.fori_loop(0, CHUNKS, drain, 0)
    pltpu.make_async_copy(gath, g_out, osem.at[0]).wait()
    pltpu.make_async_copy(codes, c_out, osem.at[1]).wait()
    pltpu.make_async_copy(low, r_out, osem.at[2]).wait()
    pltpu.make_async_copy(plow, p_out, osem.at[3]).wait()


def exchange(acts, enc, enc_bias, dec, dec_bias):
    any_spec = pl.BlockSpec(memory_space=pl.ANY)
    vmem = pl.BlockSpec(memory_space=pltpu.VMEM)
    V = pltpu.VMEM
    sums = [
        V((2, ROWS, LATS), F32), V((2, ROWS, LATS), F32),
        V((CHUNKS, ROWS, LATS), BF16), V((CHUNKS, ROWS, LATS), BF16),
        V((CHUNKS, 3, 64, LATS), BF16), V((CHUNKS, 3, 64, LATS), BF16),
        V((CHUNKS, 32, LATS), BF16), V((CHUNKS, 32, LATS), BF16),
        V((CHUNKS, 32, LATS), BF16), V((CHUNKS, 32, LATS), BF16),
        V((2, 32, LATS), F32), V((2, 32, LATS), F32), V((CHUNKS, 32, LATS), F32),
    ]
    recon = [
        V((2, ROWS, WIDTH), F32), V((CHUNKS, ROWS, WIDTH), BF16), V((CHUNKS, 128, WIDTH), BF16),
        V((CHUNKS, 3, 32, WIDTH), BF16), V((CHUNKS, 3, 32, WIDTH), BF16),
        V((CHUNKS, 16, WIDTH), BF16), V((CHUNKS, 16, WIDTH), BF16), V((2, 16, WIDTH), F32),
        V((8, LATS), F32),
    ]
    return pl.pallas_call(
        step_kernel,
        out_shape=[
            jax.ShapeDtypeStruct((CHUNKS, ROWS, WIDTH), BF16),
            jax.ShapeDtypeStruct((CHUNKS, ROWS, LATS), BF16),
            jax.ShapeDtypeStruct((CHUNKS, ROWS, WIDTH), BF16),
            jax.ShapeDtypeStruct((CHUNKS, ROWS, LATS), BF16),
            jax.ShapeDtypeStruct((LATS, 128), F32),
        ],
        in_specs=[vmem, any_spec, vmem, any_spec, vmem],
        out_specs=[any_spec, any_spec, any_spec, any_spec, vmem],
        scratch_shapes=[
            V((WIDTH, LATS), BF16), V((LATS, WIDTH), BF16),
            V((CHUNKS, ROWS, WIDTH), BF16), V((CHUNKS, ROWS, LATS), BF16),
            V((CHUNKS, ROWS, WIDTH), BF16), V((CHUNKS, ROWS, LATS), BF16),
            *sums, *recon,
            pltpu.SemaphoreType.DMA((STAGES, CHUNKS)),
            pltpu.SemaphoreType.DMA((STAGES, CHUNKS)),
            pltpu.SemaphoreType.DMA((2,)),
            pltpu.SemaphoreType.DMA((4,)),
        ],
        compiler_params=pltpu.CompilerParams(
            collective_id=0, has_side_effects=True, vmem_limit_bytes=60 << 20
        ),
        name="exchange",
    )(acts, enc, enc_bias, dec, dec_bias)


def rows_dot(left, right):
    return lax.dot_general(left, right, (((0,), (0,)), ((), ())), preferred_element_type=F32)


def enc_kernel(g, p, out, bias_out):
    out[...] = rows_dot(g[...], p[...])

    @pl.when(pl.program_id(0) == 0)
    def _():
        bias_out[...] = jnp.dot(jnp.ones((8, TOKENS), BF16), p[...], preferred_element_type=F32)


def enc_grads(g, p):
    n = 8
    w = WIDTH // n
    return pl.pallas_call(
        enc_kernel,
        grid=(n,),
        out_shape=[jax.ShapeDtypeStruct((WIDTH, LATS), F32), jax.ShapeDtypeStruct((8, LATS), F32)],
        in_specs=[
            pl.BlockSpec((TOKENS, w), lambda i: (0, i)),
            pl.BlockSpec((TOKENS, LATS), lambda i: (0, 0)),
        ],
        out_specs=[pl.BlockSpec((w, LATS), lambda i: (i, 0)), pl.BlockSpec((8, LATS), lambda i: (0, 0))],
        compiler_params=pltpu.CompilerParams(vmem_limit_bytes=56 << 20),
        name="enc_grads",
    )(g, p)


def dec_kernel(c, r, dec, norm, out, bias_out):
    sums = rows_dot(c[...], jnp.ones((TOKENS, 128), BF16))
    factor = (PENALTY * SCALE) * sums / norm[...]
    for i in range(4):
        cols = slice(i * 512, (i + 1) * 512)
        value = rows_dot(c[...], r[:, cols])
        for j in range(4):
            at = i * 4 + j
            part = value[:, j * 128 : (j + 1) * 128]
            part = part + factor * dec[:, at * 128 : (at + 1) * 128].astype(F32)
            out[pl.ds(at, part.shape[0], stride=16), :] = part

    @pl.when(pl.program_id(0) == 0)
    def _():
        bias_out[...] = jnp.dot(jnp.ones((8, TOKENS), BF16), r[...], preferred_element_type=F32)


def dec_grads(c, r, dec, norm):
    n = 4
    w = LATS // n
    return pl.pallas_call(
        dec_kernel,
        grid=(n,),
        out_shape=[jax.ShapeDtypeStruct((LATS * 16, 128), F32), jax.ShapeDtypeStruct((8, WIDTH), F32)],
        in_specs=[
            pl.BlockSpec((TOKENS, w), lambda i: (0, i)),
            pl.BlockSpec((TOKENS, WIDTH), lambda i: (0, 0)),
            pl.BlockSpec((w, WIDTH), lambda i: (i, 0)),
            pl.BlockSpec((w, 128), lambda i: (i, 0)),
        ],
        out_specs=[pl.BlockSpec((w * 16, 128), lambda i: (i, 0)), pl.BlockSpec((8, WIDTH), lambda i: (0, 0))],
        compiler_params=pltpu.CompilerParams(vmem_limit_bytes=56 << 20),
        name="dec_grads",
    )(c, r, dec, norm)


def on_device(acts, enc_weight, enc_bias, dec_weight, dec_bias):
    dec = dec_weight.reshape(LATS, WIDTH)
    g, c, r, p, norm = exchange(
        acts.reshape(TOKENS // 16, WIDTH), enc_weight.reshape(WIDTH, LATS), enc_bias.reshape(1, LATS), dec, dec_bias
    )
    g, r = g.reshape(TOKENS, WIDTH), r.reshape(TOKENS, WIDTH)
    c, p = c.reshape(TOKENS, LATS), p.reshape(TOKENS, LATS)
    dec_grad, dec_bias_grad = dec_grads(c, r, dec, norm)
    enc_grad, enc_bias_grad = enc_grads(g, p)
    return (
        enc_grad.reshape(1, WIDTH, LATS),
        enc_bias_grad[0],
        dec_grad.reshape(LATS, 1, WIDTH),
        dec_bias_grad[0:1],
    )


def solution(mesh):
    return jax.shard_map(
        on_device,
        mesh=mesh,
        in_specs=(
            P("latent", "layer", None),
            P("layer", None, "latent"),
            P("latent"),
            P("latent", "layer", None),
            P("layer", None),
        ),
        out_specs=(
            P("layer", None, "latent"),
            P("latent"),
            P("latent", "layer", None),
            P("layer", None),
        ),
        check_vma=False,
    )
```

time: 521 us -> 201 us (0.39)
  waiting for transfers between devices: 320 us -> 0 us
  Pallas kernels: 0 us -> 196 us
  blocking collectives: 104 us -> 0 us
  matrix products: 47.9 us -> 0 us
  local copies, waits for them, and re-layouts: 22.1 us -> 2.79 us
  between operations: 13.8 us -> 0.64 us
  other arithmetic: 13 us -> 0 us
    pallas_call x0 -> x3, Pallas kernels: none -> 196 us  [the longest x1 172 us: exchange(): pl.pallas_call(step_kernel, out_shape=[jax.ShapeDtypeStruct((CHUNKS, ROWS...]
    all_gather x2 -> x0, waiting for transfers between devices: 114 us -> none  [the longest x1 58 us: on_device(): gathered = lax.all_gather(own_rows, 'latent', axis=0, tiled=True)]
    psum x2 -> x0, waiting for transfers between devices: 105 us -> none  [the longest x1 105 us: on_device(): pre_sum, totals = lax.psum((pre_part, norm_part), 'layer')]
    psum x2 -> x0, blocking collectives: 104 us -> none  [the longest x1 85.2 us: on_device(): lax.psum(jnp.sum(recon_grad, axis=0), 'latent').reshape(layers_dev, width)]
    reduce_scatter x1 -> x0, waiting for transfers between devices: 101 us -> none  [on_device(): lax.psum_scatter(jnp.dot(rows, dec_flat, preferred_element_type=jnp.float...]
    dot_general x5 -> x0, matrix products: 47.9 us -> none  [the longest x2 21.3 us: contract_rows(): lax.dot_general(left, right, (((0,), (0,)), ((), ())), preferred_element_...]
    unnamed x10 -> x0, local copies, waits for them, and re-layouts: 22.1 us -> none
    reduce_sum x4 -> x0, other arithmetic: 12.9 us -> none  [the longest x1 4.96 us: on_device(): enc_bias_grad = jnp.sum(pre_grad, axis=0)]
  transfers between devices with their start and end apart: 5 -> 0, of which waited for: 4 -> 0; matrix products, arithmetic and copies ran while one was open for 5% -> 0% of each run, Pallas kernels for 0% -> 0%
where the time goes in v1:
time: 201 us; the launch traced here: 199 us
  Pallas kernels  196 us (98%)
  local copies, waits for them, and re-layouts  2.79 us (1%)
    pallas_call x1, Pallas kernels, exchange(): pl.pallas_call(step_kernel, out_shape=[jax.ShapeDtypeStruct((CHUNKS, ROWS...  172 us
    pallas_call x1, Pallas kernels, dec_grads(): pl.pallas_call(dec_kernel, grid=(n,), out_shape=[jax.ShapeDtypeStruct((LA...  12.7 us
    pallas_call x1, Pallas kernels, enc_grads(): pl.pallas_call(enc_kernel, grid=(n,), out_shape=[jax.ShapeDtypeStruct((WI...  11.2 us

profile of v1, /device:TPU:96, one launch (start us, length us, event | category | flops | bytes accessed | tf_op | source)
XLA Modules:
  0.0 199.0 jit_solution(16065763338948057261)
XLA Ops:
  0.6 171.7 %exchange.1 = (bf16[4,256,2048]{2,1,0:T(8,128)(2,1)}, bf16[4,256,1024]{2,1,0:T(8,128)(2,1)}, bf16[4,256,2048]{2,1,0:T(8,128)(2,1)}, bf16[4,256,1024]{2,1,0:T(8,128)(2,1)}, f32[1024,128]{1,0:T(8,128)}) custom-call(bf16[64,2048]{1,0:T(8,128)(2,1)} %bitcast.18, bf16[2048,1024]{1,0:T(8,128)(2,1)} %bitcast.14, f32[1,1024]{1,0:T(1,128)} %bitcast.19, ...), custom_call_target="tpu_custom_call" | custom-call | tf_op jit(solution)/shard_map/exchange/pallas_call | solution.py:357
  172.3 12.7 %dec_grads.1 = (f32[16384,128]{1,0:T(8,128)}, f32[8,2048]{1,0:T(8,128)}) custom-call(bf16[1024,1024]{1,0:T(8,128)(2,1)} %bitcast.17, bf16[1024,2048]{1,0:T(8,128)(2,1)} %bitcast.15, bf16[1024,2048]{1,0:T(8,128)(2,1)} %bitcast.12, f32[1024,128]{1,0:T(8,128)} %get-tuple-element.19.norm), custom_call_target="tpu_custom_call" | custom-call | tf_op jit(solution)/shard_map/dec_grads/pallas_call | solution.py:434
  185.0 1.4 slice.7
  186.5 11.2 %enc_grads.1 = (f32[2048,1024]{1,0:T(8,128)}, f32[8,1024]{1,0:T(8,128)}) custom-call(bf16[1024,2048]{1,0:T(8,128)(2,1)} %bitcast.13, bf16[1024,1024]{1,0:T(8,128)(2,1)} %bitcast.16), custom_call_target="tpu_custom_call" | custom-call | tf_op jit(solution)/shard_map/enc_grads/pallas_call | solution.py:400
  197.7 1.4 slice.6

commit v2 on v1

v2 whole, which is shorter than its diff:
```python
import functools
import math

import jax
import jax.numpy as jnp
from jax import lax
from jax.experimental import pallas as pl
from jax.experimental.pallas import tpu as pltpu
from jax.sharding import PartitionSpec as P

PENALTY = 0.05
EPS = 1e-06
MESH = pl.DeviceIdType.MESH
BF16 = jnp.bfloat16
F32 = jnp.float32

TOKENS = 1024
WIDTH = 2048
LATS = 1024
HALF = LATS // 2
PART = WIDTH // 2
CHUNKS = 8
ROWS = TOKENS // CHUNKS
SCALE = 1.0 / math.sqrt(TOKENS)
TILE = 512

STAGES = 18
SPAN = 1
SEMS = 25


def aligned(value, multiple):
    return pl.multiple_of(value, multiple)

CODE = 2.0**18
FLOOR = 2.0**-120


def pack(value):
    value = value * CODE
    return (value * value * (value * jnp.abs(value))).astype(BF16)


def unpack(coded):
    coded = coded.astype(F32)
    size = lax.rsqrt(lax.rsqrt(jnp.maximum(jnp.abs(coded), FLOOR))) * (1.0 / CODE)
    return jnp.where(coded < 0.0, -size, size)


def plain(value):
    return value.astype(BF16)


def widen(value):
    return value.astype(F32)


def step_kernel(
    acts, enc_hbm, enc_bias, dec_hbm, dec_bias,
    g_out, c_out, r_out, p_out, norm_out,
    enc, dec, dec_t, gath, codes, low, plow,
    sums1, sums2, active,
    full3, send3, crecv, xsend, xrecv, zsend3, zrecv3, keep3, norm_row,
    ssem, rsem, lsem, osem,
):
    a = lax.axis_index("layer")
    b = lax.axis_index("latent")
    zl, y = a // 4, a % 4
    x, zh, c = b // 4, (b // 2) % 2, b % 2

    def ydev(d):
        return (zl * 4 + (y + d) % 4, b)

    zldev = ((1 - zl) * 4 + y, b)

    def xdev(d):
        return (a, ((x + d) % 4) * 4 + zh * 2 + c)

    zhdev = (a, x * 4 + (1 - zh) * 2 + c)
    cdev = (a, x * 4 + zh * 2 + 1 - c)

    load_enc = pltpu.make_async_copy(enc_hbm, enc, lsem.at[0])
    load_dec = pltpu.make_async_copy(dec_hbm, dec, lsem.at[1])
    load_enc.start()
    load_dec.start()

    barrier = pltpu.get_barrier_semaphore()
    peers = [zldev, zhdev, cdev] + [ydev(d) for d in (1, 2, 3)] + [xdev(d) for d in (1, 2, 3)]
    for peer in peers:
        pl.semaphore_signal(barrier, inc=1, device_id=peer, device_id_type=MESH)
    pl.semaphore_wait(barrier, len(peers))

    def push(sem, k, src, dst, device):
        pltpu.make_async_remote_copy(
            src_ref=src, dst_ref=dst, send_sem=ssem.at[sem, k], recv_sem=rsem.at[sem, k],
            device_id=device, device_id_type=MESH,
        ).start()

    def arrived(sem, k, ref):
        pltpu.make_async_copy(ref, ref, rsem.at[sem, k]).wait()

    def gone(sem, k, ref):
        pltpu.make_async_copy(ref, ref, ssem.at[sem, k]).wait()

    left, right = pl.ds(0, HALF), pl.ds(HALF, HALF)
    mine = pl.ds(aligned(zh * PART, PART), PART)
    theirs = pl.ds(aligned((1 - zh) * PART, PART), PART)

    def sum_send(sem, k, bufs):
        send, ya, zb = bufs["send"], bufs["ya"], bufs["zb"]
        push(sem + 1, k, send.at[k, :, 1 - zl, :, right], zb.at[k], zldev)
        for d in (1, 2, 3):
            push(sem, k, send.at[k, (y + d) % 4, :, :, left], ya.at[k, d - 1], ydev(d))

    def sum_mid(sem, k, bufs, narrow, wide):
        full, ya, zb, za_send, za, mid, mid_f32, yb, keep = (
            bufs[n] for n in ("full", "ya", "zb", "za_send", "za", "mid", "mid_f32", "yb", "keep")
        )
        arrived(sem + 1, k, zb.at[k])
        value = full[k % 2, :, zl, :, right] + wide(zb[k])
        mid_f32[k % 2] = value
        mid[k] = narrow(value)
        for d in (1, 2, 3):
            push(sem + 3, k, mid.at[k, (y + d) % 4], yb.at[k, d - 1], ydev(d))
        arrived(sem, k, ya.at[k])

        def total(half):
            value = full[k % 2, y, half, :, left]
            for d in range(3):
                value = value + wide(ya[k, d, half])
            return value

        za_send[k] = narrow(total(1 - zl))
        push(sem + 2, k, za_send.at[k], za.at[k], zldev)
        keep[k % 2] = total(zl)

    def sum_end(sem, k, bufs, wide):
        za, mid_f32, yb, keep = (bufs[n] for n in ("za", "mid_f32", "yb", "keep"))
        arrived(sem + 3, k, yb.at[k])
        second = mid_f32[k % 2, y]
        for d in range(3):
            second = second + wide(yb[k, d])
        arrived(sem + 2, k, za.at[k])
        return keep[k % 2] + wide(za[k]), second

    def spread_send(sem, k, buf):
        first, second = buf.at[k, y, zl, :, left], buf.at[k, y, zl, :, right]
        push(sem, k, first, first, zldev)
        for d in (1, 2, 3):
            push(sem + 2, k, second, second, ydev(d))
            push(sem + 1, k, first, first, ydev(d))

    def spread_mid(sem, k, buf):
        first = buf.at[k, y, 1 - zl, :, left]
        arrived(sem, k, first)
        for d in (1, 2, 3):
            push(sem + 1, k, first, first, ydev(d))
        arrived(sem + 2, k, buf.at[k, pl.ds(0, 3), 0, :, right])
        column = buf.at[k, :, zl, :, right]
        push(sem + 3, k, column, column, zldev)

    def spread_end(sem, k, buf):
        arrived(sem + 1, k, buf.at[k, pl.ds(0, 3), :, :, left])
        arrived(sem + 3, k, buf.at[k, :, 0, :, right])

    def even(stage):
        def run(k):
            pl.when(k % 2 == 0)(functools.partial(stage, k))

        return run

    def m0(k):
        gath[k + zh, c, x] = acts[pl.ds(aligned(k * 8, 16), 16), :]
        ref = gath.at[k + zh, c, x]
        push(0, k, ref, ref, zhdev)
        for d in (1, 2, 3):
            push(1, k, ref, ref, xdev(d))

    def m1(k):
        ref = gath.at[k + 1 - zh, c, x]
        arrived(0, k, ref)
        for d in (1, 2, 3):
            push(1, k, ref, ref, xdev(d))

    def m2(k):
        arrived(1, k, gath.at[pl.ds(k, 2), 0, pl.ds(0, 3)])
        ref = gath.at[pl.ds(k, 2), c]
        push(2, k, ref, ref, cdev)

    def wait_pair(k):
        arrived(2, k, gath.at[pl.ds(k, 2), 1 - c])

    def m3(k):
        even(wait_pair)(k)
        pltpu.make_async_copy(gath.at[k], g_out.at[k], osem.at[0]).start()

        def tile(n, _):
            cols = pl.ds(aligned(n * TILE, TILE), TILE)
            left_rows = gath[k].reshape(ROWS, WIDTH)
            value = jnp.dot(left_rows, enc[:, cols], preferred_element_type=F32).reshape(4, 2, 16, TILE)
            sums1["full"][k % 2, :, :, :, cols] = value
            sums1["send"][k, :, :, :, cols] = pack(value)
            return 0

        lax.fori_loop(0, LATS // TILE, tile, 0)
        sum_send(3, k, sums1)

    def m4(k):
        sum_mid(3, k, sums1, pack, unpack)

    def m5(k):
        for value, cols in zip(sum_end(3, k, sums1, unpack), (left, right)):
            value = jnp.maximum(value + enc_bias[:, cols], 0.0)
            active[k, :, cols] = value
            codes[k, y, zl, :, cols] = (value * value).astype(BF16)
        spread_send(7, k, codes)

    def m6(k):
        spread_mid(7, k, codes)

    def m7(k):
        spread_end(7, k, codes)
        pltpu.make_async_copy(codes.at[k], c_out.at[k], osem.at[1]).start()

        def tile(n, _):
            cols = pl.ds(aligned(n * TILE, TILE), TILE)
            rows = codes[k].reshape(ROWS, LATS)
            value = jnp.dot(rows, dec[:, cols], preferred_element_type=F32).reshape(2, 4, 16, TILE)
            full3[k % 2, :, :, :, cols] = value
            send3[k, :, :, :, cols] = value.astype(BF16)
            return 0

        lax.fori_loop(0, WIDTH // TILE, tile, 0)
        push(11, k, send3.at[k, 1 - c], crecv.at[k], cdev)

    def m8(k):
        arrived(11, k, crecv.at[k])
        for d in (1, 2, 3):
            to = (x + d) % 4
            xsend[k, d - 1] = (full3[k % 2, c, to] + crecv[k, to].astype(F32)).astype(BF16)
            push(12, k, xsend.at[k, d - 1], xrecv.at[k, d - 1], xdev(d))

    def m9(k):
        arrived(12, k, xrecv.at[k])

        def total(cols):
            value = full3[k % 2, c, x, :, cols] + crecv[k, x, :, cols].astype(F32)
            for d in range(3):
                value = value + xrecv[k, d, :, cols].astype(F32)
            return value

        zsend3[k] = total(theirs).astype(BF16)
        push(13, k, zsend3.at[k], zrecv3.at[k], zhdev)
        keep3[k % 2] = total(mine)

    def m10(k):
        arrived(13, k, zrecv3.at[k])
        recon = keep3[k % 2] + zrecv3[k].astype(F32) + dec_bias[:, mine]
        flat = gath[k, c, x, :, mine].astype(F32)
        low[k, c, x, :, mine] = ((recon - flat) * SCALE).astype(BF16)
        ref = low.at[k, c, x, :, mine]
        push(14, k, ref, ref, zhdev)
        for d in (1, 2, 3):
            push(15, k, ref, ref, xdev(d))

    def m11(k):
        ref = low.at[k, c, x, :, theirs]
        arrived(14, k, ref)
        for d in (1, 2, 3):
            push(15, k, ref, ref, xdev(d))

    def m12(k):
        arrived(15, k, low.at[k, 0, pl.ds(0, 3)])
        ref = low.at[k, c]
        push(16, k, ref, ref, cdev)

    def m13(k):
        arrived(16, k, low.at[k, 1 - c])
        pltpu.make_async_copy(low.at[k], r_out.at[k], osem.at[2]).start()

        def tile(n, _):
            cols = pl.ds(aligned(n * TILE, TILE), TILE)
            rows = low[k].reshape(ROWS, WIDTH)
            value = jnp.dot(rows, dec_t[:, cols], preferred_element_type=F32)
            value = (value + (PENALTY * SCALE) * norm_row[0:1, cols]).reshape(4, 2, 16, TILE)
            sums2["full"][k % 2, :, :, :, cols] = value
            sums2["send"][k, :, :, :, cols] = value.astype(BF16)
            return 0

        lax.fori_loop(0, LATS // TILE, tile, 0)
        sum_send(17, k, sums2)

    def m14(k):
        sum_mid(17, k, sums2, plain, widen)

    def m15(k):
        for value, cols in zip(sum_end(17, k, sums2, widen), (left, right)):
            plow[k, y, zl, :, cols] = (value * (2.0 * active[k, :, cols])).astype(BF16)
        spread_send(21, k, plow)

    def m16(k):
        spread_mid(21, k, plow)

    def m17(k):
        spread_end(21, k, plow)
        pltpu.make_async_copy(plow.at[k], p_out.at[k], osem.at[3]).start()

    def prepare(n):
        rows = pl.ds(aligned(n * 128, 128), 128)
        block = dec[rows, :]
        value = block.astype(F32)
        norm = jnp.sqrt(jnp.sum(value * value, axis=1, keepdims=True) + EPS)
        wide = jnp.broadcast_to(norm, (128, 128))
        norm_out[rows, :] = wide
        norm_row[:, rows] = wide.T[0:8, :]
        dec_t[:, rows] = block.T

    stages = [even(m0), even(m1), even(m2), m3, m4, m5, m6, m7, m8, m9, m10, m11, m12, m13, m14, m15, m16, m17]

    def iteration(t, _):
        for place in range(SPAN):
            for m in reversed(range(place, STAGES, SPAN)):
                k = t - m // SPAN
                pl.when(jnp.logical_and(k >= 0, k < CHUNKS))(functools.partial(stages[m], k))
            if place == 0:

                @pl.when(t == 0)
                def _():
                    load_enc.wait()
                    load_dec.wait()

                @pl.when(t < 4)
                def _():
                    prepare(2 * t)
                    prepare(2 * t + 1)

        return 0

    lax.fori_loop(0, CHUNKS + (STAGES - 1) // SPAN, iteration, 0)

    def drain(k, _):
        @pl.when(k % 2 == 0)
        def _():
            gone(0, k, gath.at[k, 0, 0])
            gone(1, k, gath.at[pl.ds(k, 2), 0, pl.ds(0, 3)])
            gone(2, k, gath.at[pl.ds(k, 2), 0])

        for sem, bufs in ((3, sums1), (17, sums2)):
            gone(sem, k, bufs["ya"].at[k])
            gone(sem + 1, k, bufs["zb"].at[k])
            gone(sem + 2, k, bufs["za"].at[k])
            gone(sem + 3, k, bufs["yb"].at[k])
        for sem, buf in ((7, codes), (21, plow)):
            gone(sem, k, buf.at[k, 0, 0, :, left])
            gone(sem + 1, k, buf.at[k, pl.ds(0, 3), :, :, left])
            gone(sem + 2, k, buf.at[k, pl.ds(0, 3), 0, :, left])
            gone(sem + 3, k, buf.at[k, :, 0, :, left])
        gone(11, k, crecv.at[k])
        gone(12, k, xsend.at[k])
        gone(13, k, zsend3.at[k])
        gone(14, k, zsend3.at[k])
        gone(15, k, low.at[k, 0, pl.ds(0, 3)])
        gone(16, k, low.at[k, 0])
        return 0

    lax.fori_loop(0, CHUNKS, drain, 0)
    pltpu.make_async_copy(gath, g_out, osem.at[0]).wait()
    pltpu.make_async_copy(codes, c_out, osem.at[1]).wait()
    pltpu.make_async_copy(low, r_out, osem.at[2]).wait()
    pltpu.make_async_copy(plow, p_out, osem.at[3]).wait()


def layer_sum():
    V = pltpu.VMEM
    return {
        "full": V((2, 4, 2, 16, LATS), F32),
        "send": V((CHUNKS, 4, 2, 16, LATS), BF16),
        "ya": V((CHUNKS, 3, 2, 16, HALF), BF16),
        "zb": V((CHUNKS, 4, 16, HALF), BF16),
        "za_send": V((CHUNKS, 16, HALF), BF16),
        "za": V((CHUNKS, 16, HALF), BF16),
        "mid": V((CHUNKS, 4, 16, HALF), BF16),
        "mid_f32": V((2, 4, 16, HALF), F32),
        "yb": V((CHUNKS, 3, 16, HALF), BF16),
        "keep": V((2, 16, HALF), F32),
    }


def exchange(acts, enc, enc_bias, dec, dec_bias):
    any_spec = pl.BlockSpec(memory_space=pl.ANY)
    vmem = pl.BlockSpec(memory_space=pltpu.VMEM)
    V = pltpu.VMEM
    by_latent = (CHUNKS, 2, 4, 16, WIDTH)
    by_layer = (CHUNKS, 4, 2, 16, LATS)
    return pl.pallas_call(
        step_kernel,
        out_shape=[
            jax.ShapeDtypeStruct(by_latent, BF16),
            jax.ShapeDtypeStruct(by_layer, BF16),
            jax.ShapeDtypeStruct(by_latent, BF16),
            jax.ShapeDtypeStruct(by_layer, BF16),
            jax.ShapeDtypeStruct((LATS, 128), F32),
        ],
        in_specs=[vmem, any_spec, vmem, any_spec, vmem],
        out_specs=[any_spec, any_spec, any_spec, any_spec, vmem],
        scratch_shapes=[
            V((WIDTH, LATS), BF16), V((LATS, WIDTH), BF16), V((WIDTH, LATS), BF16),
            V(by_latent, BF16), V(by_layer, BF16), V(by_latent, BF16), V(by_layer, BF16),
            layer_sum(), layer_sum(), V((CHUNKS, 16, LATS), F32),
            V((2, 2, 4, 16, WIDTH), F32), V(by_latent, BF16), V((CHUNKS, 4, 16, WIDTH), BF16),
            V((CHUNKS, 3, 16, WIDTH), BF16), V((CHUNKS, 3, 16, WIDTH), BF16),
            V((CHUNKS, 16, PART), BF16), V((CHUNKS, 16, PART), BF16), V((2, 16, PART), F32),
            V((8, LATS), F32),
            pltpu.SemaphoreType.DMA((SEMS, CHUNKS)),
            pltpu.SemaphoreType.DMA((SEMS, CHUNKS)),
            pltpu.SemaphoreType.DMA((2,)),
            pltpu.SemaphoreType.DMA((4,)),
        ],
        compiler_params=pltpu.CompilerParams(
            collective_id=0, has_side_effects=True, vmem_limit_bytes=60 << 20
        ),
        name="exchange",
    )(acts, enc, enc_bias, dec, dec_bias)


def rows_dot(left, right):
    return lax.dot_general(left, right, (((0,), (0,)), ((), ())), preferred_element_type=F32)


def enc_kernel(g, p, out, bias_out):
    out[...] = rows_dot(g[...], p[...])

    @pl.when(pl.program_id(0) == 0)
    def _():
        bias_out[...] = jnp.dot(jnp.ones((8, TOKENS), BF16), p[...], preferred_element_type=F32)


def enc_grads(g, p):
    n = 8
    w = WIDTH // n
    return pl.pallas_call(
        enc_kernel,
        grid=(n,),
        out_shape=[jax.ShapeDtypeStruct((WIDTH, LATS), F32), jax.ShapeDtypeStruct((8, LATS), F32)],
        in_specs=[
            pl.BlockSpec((TOKENS, w), lambda i: (0, i)),
            pl.BlockSpec((TOKENS, LATS), lambda i: (0, 0)),
        ],
        out_specs=[pl.BlockSpec((w, LATS), lambda i: (i, 0)), pl.BlockSpec((8, LATS), lambda i: (0, 0))],
        compiler_params=pltpu.CompilerParams(vmem_limit_bytes=56 << 20),
        name="enc_grads",
    )(g, p)


def dec_kernel(c, r, dec, norm, out, bias_out):
    sums = rows_dot(c[...], jnp.ones((TOKENS, 128), BF16))
    factor = (PENALTY * SCALE) * sums / norm[...]
    for i in range(4):
        cols = slice(i * 512, (i + 1) * 512)
        value = rows_dot(c[...], r[:, cols])
        for j in range(4):
            at = i * 4 + j
            part = value[:, j * 128 : (j + 1) * 128]
            part = part + factor * dec[:, at * 128 : (at + 1) * 128].astype(F32)
            out[pl.ds(at, part.shape[0], stride=16), :] = part

    @pl.when(pl.program_id(0) == 0)
    def _():
        bias_out[...] = jnp.dot(jnp.ones((8, TOKENS), BF16), r[...], preferred_element_type=F32)


def dec_grads(c, r, dec, norm):
    n = 4
    w = LATS // n
    return pl.pallas_call(
        dec_kernel,
        grid=(n,),
        out_shape=[jax.ShapeDtypeStruct((LATS * 16, 128), F32), jax.ShapeDtypeStruct((8, WIDTH), F32)],
        in_specs=[
            pl.BlockSpec((TOKENS, w), lambda i: (0, i)),
            pl.BlockSpec((TOKENS, WIDTH), lambda i: (0, 0)),
            pl.BlockSpec((w, WIDTH), lambda i: (i, 0)),
            pl.BlockSpec((w, 128), lambda i: (i, 0)),
        ],
        out_specs=[pl.BlockSpec((w * 16, 128), lambda i: (i, 0)), pl.BlockSpec((8, WIDTH), lambda i: (0, 0))],
        compiler_params=pltpu.CompilerParams(vmem_limit_bytes=56 << 20),
        name="dec_grads",
    )(c, r, dec, norm)


def on_device(acts, enc_weight, enc_bias, dec_weight, dec_bias):
    dec = dec_weight.reshape(LATS, WIDTH)
    g, c, r, p, norm = exchange(
        acts.reshape(TOKENS // 16, WIDTH), enc_weight.reshape(WIDTH, LATS), enc_bias.reshape(1, LATS), dec, dec_bias
    )
    g, r = g.reshape(TOKENS, WIDTH), r.reshape(TOKENS, WIDTH)
    c, p = c.reshape(TOKENS, LATS), p.reshape(TOKENS, LATS)
    dec_grad, dec_bias_grad = dec_grads(c, r, dec, norm)
    enc_grad, enc_bias_grad = enc_grads(g, p)
    return (
        enc_grad.reshape(1, WIDTH, LATS),
        enc_bias_grad[0],
        dec_grad.reshape(LATS, 1, WIDTH),
        dec_bias_grad[0:1],
    )


def solution(mesh):
    return jax.shard_map(
        on_device,
        mesh=mesh,
        in_specs=(
            P("latent", "layer", None),
            P("layer", None, "latent"),
            P("latent"),
            P("latent", "layer", None),
            P("layer", None),
        ),
        out_specs=(
            P("layer", None, "latent"),
            P("latent"),
            P("latent", "layer", None),
            P("layer", None),
        ),
        check_vma=False,
    )
```

time: 201 us -> 154 us (0.77)
  Pallas kernels: 196 us -> 148 us
    pallas_call x1, Pallas kernels: 172 us -> 124 us  [exchange(): pl.pallas_call(step_kernel, out_shape=[jax.ShapeDtypeStruct(by_latent, BF...]
where the time goes in v2:
time: 154 us; the launch traced here: 152 us
  Pallas kernels  148 us (96%)
  local copies, waits for them, and re-layouts  2.79 us (2%)
    pallas_call x1, Pallas kernels, exchange(): pl.pallas_call(step_kernel, out_shape=[jax.ShapeDtypeStruct(by_latent, BF...  124 us
    pallas_call x1, Pallas kernels, dec_grads(): pl.pallas_call(dec_kernel, grid=(n,), out_shape=[jax.ShapeDtypeStruct((LA...  12.7 us
    pallas_call x1, Pallas kernels, enc_grads(): pl.pallas_call(enc_kernel, grid=(n,), out_shape=[jax.ShapeDtypeStruct((WI...  11.2 us

profile of v2, /device:TPU:96, one launch (start us, length us, event | category | flops | bytes accessed | tf_op | source)
XLA Modules:
  0.0 151.7 jit_solution(11880696013501967084)
XLA Ops:
  0.6 124.3 %exchange.1 = (bf16[8,2,4,16,2048]{4,3,2,1,0:T(8,128)(2,1)}, bf16[8,4,2,16,1024]{4,3,2,1,0:T(8,128)(2,1)}, bf16[8,2,4,16,2048]{4,3,2,1,0:T(8,128)(2,1)}, bf16[8,4,2,16,1024]{4,3,2,1,0:T(8,128)(2,1)}, f32[1024,128]{1,0:T(8,128)}) custom-call(bf16[64,2048]{1,0:T(8,128)(2,1)} %bitcast.18, bf16[2048,1024]{1,0:T(8,128)(2,1)} %bitcast.14, f32[1,1024]{1,0:T(1,128)} %bitcast.19, ...), custom_call_target="tpu_custom_call" | custom-call | tf_op jit(solution)/shard_map/exchange/pallas_call | solution.py:395
  125.0 12.7 %dec_grads.1 = (f32[16384,128]{1,0:T(8,128)}, f32[8,2048]{1,0:T(8,128)}) custom-call(bf16[1024,1024]{1,0:T(8,128)(2,1)} %bitcast.17, bf16[1024,2048]{1,0:T(8,128)(2,1)} %bitcast.15, bf16[1024,2048]{1,0:T(8,128)(2,1)} %bitcast.12, f32[1024,128]{1,0:T(8,128)} %get-tuple-element.19.norm), custom_call_target="tpu_custom_call" | custom-call | tf_op jit(solution)/shard_map/dec_grads/pallas_call | solution.py:475
  137.7 1.4 slice.7
  139.2 11.2 %enc_grads.1 = (f32[2048,1024]{1,0:T(8,128)}, f32[8,1024]{1,0:T(8,128)}) custom-call(bf16[1024,2048]{1,0:T(8,128)(2,1)} %bitcast.13, bf16[1024,1024]{1,0:T(8,128)(2,1)} %bitcast.16), custom_call_target="tpu_custom_call" | custom-call | tf_op jit(solution)/shard_map/enc_grads/pallas_call | solution.py:441
  150.4 1.4 slice.6

commit v3 on v2

--- a/solution.py
+++ b/solution.py
@@ -24,9 +24,23 @@
 SCALE = 1.0 / math.sqrt(TOKENS)
 TILE = 512
 
-STAGES = 18
-SPAN = 1
 SEMS = 25
+
+HOPS = (1.0,) * 17
+STARTS = tuple(sum(HOPS[:m]) for m in range(len(HOPS) + 1))
+LAGS = tuple(int(start) for start in STARTS)
+ORDER = tuple(sorted(range(len(STARTS)), key=lambda m: (STARTS[m] % 1.0, -m)))
+
+
+def before(first, second, ahead):
+    at = (LAGS[first], ORDER.index(first))
+    return at < (LAGS[second] + ahead, ORDER.index(second))
+
+
+FULL = CHUNKS - 1 + LAGS[13]
+assert FULL + 4 <= CHUNKS + LAGS[-1]
+assert all(before(m, m + 1, 0) for m in range(len(HOPS)))
+assert all(before(last, first, 2) for first, last in ((3, 4), (4, 5), (7, 9), (9, 10), (13, 14), (14, 15)))
 
 
 def aligned(value, multiple):
@@ -57,10 +71,10 @@
 
 def step_kernel(
     acts, enc_hbm, enc_bias, dec_hbm, dec_bias,
-    g_out, c_out, r_out, p_out, norm_out,
+    g_out, p_out, d_out, low_sum, plow_sum,
     enc, dec, dec_t, gath, codes, low, plow,
     sums1, sums2, active,
-    full3, send3, crecv, xsend, xrecv, zsend3, zrecv3, keep3, norm_row,
+    full3, send3, crecv, xsend, xrecv, zsend3, zrecv3, keep3, norm_row, norm_wide, factor, code_sum, products,
     ssem, rsem, lsem, osem,
 ):
     a = lax.axis_index("layer")
@@ -103,6 +117,7 @@
         pltpu.make_async_copy(ref, ref, ssem.at[sem, k]).wait()
 
     left, right = pl.ds(0, HALF), pl.ds(HALF, HALF)
+    lower, upper = pl.ds(0, PART), pl.ds(PART, PART)
     mine = pl.ds(aligned(zh * PART, PART), PART)
     theirs = pl.ds(aligned((1 - zh) * PART, PART), PART)
 
@@ -144,45 +159,41 @@
         return keep[k % 2] + wide(za[k]), second
 
     def spread_send(sem, k, buf):
-        first, second = buf.at[k, y, zl, :, left], buf.at[k, y, zl, :, right]
+        own, first = buf.at[k, y, zl], buf.at[k, y, zl, :, left]
         push(sem, k, first, first, zldev)
         for d in (1, 2, 3):
-            push(sem + 2, k, second, second, ydev(d))
-            push(sem + 1, k, first, first, ydev(d))
+            push(sem + 2, k, own, own, ydev(d))
 
     def spread_mid(sem, k, buf):
         first = buf.at[k, y, 1 - zl, :, left]
         arrived(sem, k, first)
         for d in (1, 2, 3):
             push(sem + 1, k, first, first, ydev(d))
-        arrived(sem + 2, k, buf.at[k, pl.ds(0, 3), 0, :, right])
+        arrived(sem + 2, k, buf.at[k, pl.ds(0, 3), 0])
         column = buf.at[k, :, zl, :, right]
         push(sem + 3, k, column, column, zldev)
 
     def spread_end(sem, k, buf):
-        arrived(sem + 1, k, buf.at[k, pl.ds(0, 3), :, :, left])
+        arrived(sem + 1, k, buf.at[k, pl.ds(0, 3), 0, :, left])
         arrived(sem + 3, k, buf.at[k, :, 0, :, right])
 
-    def even(stage):
-        def run(k):
-            pl.when(k % 2 == 0)(functools.partial(stage, k))
-
-        return run
-
-    def m0(k):
+    def m0(pair):
+        k = 2 * pair
         gath[k + zh, c, x] = acts[pl.ds(aligned(k * 8, 16), 16), :]
         ref = gath.at[k + zh, c, x]
         push(0, k, ref, ref, zhdev)
         for d in (1, 2, 3):
             push(1, k, ref, ref, xdev(d))
 
-    def m1(k):
+    def m1(pair):
+        k = 2 * pair
         ref = gath.at[k + 1 - zh, c, x]
         arrived(0, k, ref)
         for d in (1, 2, 3):
             push(1, k, ref, ref, xdev(d))
 
-    def m2(k):
+    def m2(pair):
+        k = 2 * pair
         arrived(1, k, gath.at[pl.ds(k, 2), 0, pl.ds(0, 3)])
         ref = gath.at[pl.ds(k, 2), c]
         push(2, k, ref, ref, cdev)
@@ -191,7 +202,7 @@
         arrived(2, k, gath.at[pl.ds(k, 2), 1 - c])
 
     def m3(k):
-        even(wait_pair)(k)
+        pl.when(k % 2 == 0)(functools.partial(wait_pair, k))
         pltpu.make_async_copy(gath.at[k], g_out.at[k], osem.at[0]).start()
 
         def tile(n, _):
@@ -218,9 +229,12 @@
     def m6(k):
         spread_mid(7, k, codes)
 
+    def add_rows(total, k, rows):
+        part = jnp.sum(rows.astype(F32).reshape(ROWS // 8, 8, rows.shape[1]), axis=0)
+        total[...] = jnp.where(k == 0, part, total[...] + part)
+
     def m7(k):
         spread_end(7, k, codes)
-        pltpu.make_async_copy(codes.at[k], c_out.at[k], osem.at[1]).start()
 
         def tile(n, _):
             cols = pl.ds(aligned(n * TILE, TILE), TILE)
@@ -232,6 +246,12 @@
 
         lax.fori_loop(0, WIDTH // TILE, tile, 0)
         push(11, k, send3.at[k, 1 - c], crecv.at[k], cdev)
+        add_rows(code_sum, k, codes[k].reshape(ROWS, LATS))
+
+        @pl.when(k == CHUNKS - 1)
+        def _():
+            total = jnp.sum(code_sum[...], axis=0, keepdims=True) * (PENALTY * SCALE)
+            factor[...] = jnp.broadcast_to(total, (128, LATS)).T / norm_wide[...]
 
     def m8(k):
         arrived(11, k, crecv.at[k])
@@ -276,7 +296,6 @@
 
     def m13(k):
         arrived(16, k, low.at[k, 1 - c])
-        pltpu.make_async_copy(low.at[k], r_out.at[k], osem.at[2]).start()
 
         def tile(n, _):
             cols = pl.ds(aligned(n * TILE, TILE), TILE)
@@ -289,6 +308,7 @@
 
         lax.fori_loop(0, LATS // TILE, tile, 0)
         sum_send(17, k, sums2)
+        add_rows(low_sum, k, low[k].reshape(ROWS, WIDTH))
 
     def m14(k):
         sum_mid(17, k, sums2, plain, widen)
@@ -303,7 +323,8 @@
 
     def m17(k):
         spread_end(21, k, plow)
-        pltpu.make_async_copy(plow.at[k], p_out.at[k], osem.at[3]).start()
+        pltpu.make_async_copy(plow.at[k], p_out.at[k], osem.at[1]).start()
+        add_rows(plow_sum, k, plow[k].reshape(ROWS, LATS))
 
     def prepare(n):
         rows = pl.ds(aligned(n * 128, 128), 128)
@@ -311,32 +332,45 @@
         value = block.astype(F32)
         norm = jnp.sqrt(jnp.sum(value * value, axis=1, keepdims=True) + EPS)
         wide = jnp.broadcast_to(norm, (128, 128))
-        norm_out[rows, :] = wide
+        norm_wide[rows, :] = wide
         norm_row[:, rows] = wide.T[0:8, :]
         dec_t[:, rows] = block.T
 
-    stages = [even(m0), even(m1), even(m2), m3, m4, m5, m6, m7, m8, m9, m10, m11, m12, m13, m14, m15, m16, m17]
+    def decoder_product(n):
+        rows = pl.ds(aligned(n * (LATS // 4), LATS // 4), LATS // 4)
+        left_side = codes[:, :, :, :, rows].reshape(TOKENS, LATS // 4)
+        for half in (lower, upper):
+            right_side = low[:, :, :, :, half].reshape(TOKENS, PART)
+            value = rows_dot(left_side, right_side)
+            penalty = jnp.tile(factor[rows, :], (1, PART // 128)) * dec[rows, half].astype(F32)
+            products[rows, half] = (value + penalty).astype(BF16)
+        pltpu.make_async_copy(products.at[rows], d_out.at[rows], osem.at[2]).start()
+
+    stages = [m0, m1, m2, m3, m4, m5, m6, m7, m8, m9, m10, m11, m12, m13, m14, m15, m16, m17]
 
     def iteration(t, _):
-        for place in range(SPAN):
-            for m in reversed(range(place, STAGES, SPAN)):
-                k = t - m // SPAN
-                pl.when(jnp.logical_and(k >= 0, k < CHUNKS))(functools.partial(stages[m], k))
-            if place == 0:
-
-                @pl.when(t == 0)
-                def _():
-                    load_enc.wait()
-                    load_dec.wait()
-
-                @pl.when(t < 4)
-                def _():
-                    prepare(2 * t)
-                    prepare(2 * t + 1)
+        for m in ORDER:
+            k = t - LAGS[m]
+            if m == 3:
+                pl.when(k == 0)(load_enc.wait)
+            ready = jnp.logical_and(k >= 0, k < CHUNKS)
+            if m < 3:
+                ready = jnp.logical_and(ready, k % 2 == 0)
+            pl.when(ready)(functools.partial(stages[m], k // 2 if m < 3 else k))
+        @pl.when(jnp.logical_and(t >= FULL, t < FULL + 4))
+        def _():
+            decoder_product(t - FULL)
+
+        pl.when(t == 0)(load_dec.wait)
+
+        @pl.when(t < 4)
+        def _():
+            prepare(2 * t)
+            prepare(2 * t + 1)
 
         return 0
 
-    lax.fori_loop(0, CHUNKS + (STAGES - 1) // SPAN, iteration, 0)
+    lax.fori_loop(0, CHUNKS + LAGS[-1], iteration, 0)
 
     def drain(k, _):
         @pl.when(k % 2 == 0)
@@ -352,8 +386,8 @@
             gone(sem + 3, k, bufs["yb"].at[k])
         for sem, buf in ((7, codes), (21, plow)):
             gone(sem, k, buf.at[k, 0, 0, :, left])
-            gone(sem + 1, k, buf.at[k, pl.ds(0, 3), :, :, left])
-            gone(sem + 2, k, buf.at[k, pl.ds(0, 3), 0, :, left])
+            gone(sem + 1, k, buf.at[k, pl.ds(0, 3), 0, :, left])
+            gone(sem + 2, k, buf.at[k, pl.ds(0, 3), 0])
             gone(sem + 3, k, buf.at[k, :, 0, :, left])
         gone(11, k, crecv.at[k])
         gone(12, k, xsend.at[k])
@@ -365,9 +399,8 @@
 
     lax.fori_loop(0, CHUNKS, drain, 0)
     pltpu.make_async_copy(gath, g_out, osem.at[0]).wait()
-    pltpu.make_async_copy(codes, c_out, osem.at[1]).wait()
-    pltpu.make_async_copy(low, r_out, osem.at[2]).wait()
-    pltpu.make_async_copy(plow, p_out, osem.at[3]).wait()
+    pltpu.make_async_copy(plow, p_out, osem.at[1]).wait()
+    pltpu.make_async_copy(products, d_out, osem.at[2]).wait()
 
 
 def layer_sum():
@@ -397,12 +430,12 @@
         out_shape=[
             jax.ShapeDtypeStruct(by_latent, BF16),
             jax.ShapeDtypeStruct(by_layer, BF16),
-            jax.ShapeDtypeStruct(by_latent, BF16),
-            jax.ShapeDtypeStruct(by_layer, BF16),
-            jax.ShapeDtypeStruct((LATS, 128), F32),
+            jax.ShapeDtypeStruct((LATS, WIDTH), BF16),
+            jax.ShapeDtypeStruct((8, WIDTH), F32),
+            jax.ShapeDtypeStruct((8, LATS), F32),
         ],
         in_specs=[vmem, any_spec, vmem, any_spec, vmem],
-        out_specs=[any_spec, any_spec, any_spec, any_spec, vmem],
+        out_specs=[any_spec, any_spec, any_spec, vmem, vmem],
         scratch_shapes=[
             V((WIDTH, LATS), BF16), V((LATS, WIDTH), BF16), V((WIDTH, LATS), BF16),
             V(by_latent, BF16), V(by_layer, BF16), V(by_latent, BF16), V(by_layer, BF16),
@@ -410,11 +443,12 @@
             V((2, 2, 4, 16, WIDTH), F32), V(by_latent, BF16), V((CHUNKS, 4, 16, WIDTH), BF16),
             V((CHUNKS, 3, 16, WIDTH), BF16), V((CHUNKS, 3, 16, WIDTH), BF16),
             V((CHUNKS, 16, PART), BF16), V((CHUNKS, 16, PART), BF16), V((2, 16, PART), F32),
-            V((8, LATS), F32),
+            V((8, LATS), F32), V((LATS, 128), F32), V((LATS, 128), F32), V((8, LATS), F32),
+            V((LATS, WIDTH), BF16),
             pltpu.SemaphoreType.DMA((SEMS, CHUNKS)),
             pltpu.SemaphoreType.DMA((SEMS, CHUNKS)),
             pltpu.SemaphoreType.DMA((2,)),
-            pltpu.SemaphoreType.DMA((4,)),
+            pltpu.SemaphoreType.DMA((3,)),
         ],
         compiler_params=pltpu.CompilerParams(
             collective_id=0, has_side_effects=True, vmem_limit_bytes=60 << 20
@@ -427,81 +461,93 @@
     return lax.dot_general(left, right, (((0,), (0,)), ((), ())), preferred_element_type=F32)
 
 
-def enc_kernel(g, p, out, bias_out):
-    out[...] = rows_dot(g[...], p[...])
-
-    @pl.when(pl.program_id(0) == 0)
-    def _():
-        bias_out[...] = jnp.dot(jnp.ones((8, TOKENS), BF16), p[...], preferred_element_type=F32)
-
-
-def enc_grads(g, p):
-    n = 8
-    w = WIDTH // n
+TILES = 4
+
+
+def finish_kernel(
+    g_hbm, p_hbm, d_hbm, low_sum, plow_sum,
+    enc_out, enc_bias_out, dec_out, dec_bias_out,
+    g, p, d, enc_stage, dec_stage, lsem, gsem, dsem, esem, wsem,
+):
+    wide, tall = WIDTH // TILES, LATS // TILES
+    load_p = pltpu.make_async_copy(p_hbm, p, lsem.at[0])
+    load_g, load_d = [], []
+    for i in range(TILES):
+        cols, rows = pl.ds(i * wide, wide), pl.ds(i * tall, tall)
+        load_g.append(pltpu.make_async_copy(g_hbm.at[:, cols], g.at[:, cols], gsem.at[i]))
+        load_d.append(pltpu.make_async_copy(d_hbm.at[rows], d.at[rows], dsem.at[i]))
+    load_d[0].start()
+    load_p.start()
+    load_g[0].start()
+    enc_bias_out[...] = jnp.sum(plow_sum[...], axis=0, keepdims=True)
+    dec_bias_out[...] = jnp.sum(low_sum[...], axis=0, keepdims=True)
+    writes = []
+
+    def write(src, dst, sem):
+        writes.append(pltpu.make_async_copy(src, dst, sem))
+        writes[-1].start()
+
+    for i in range(TILES):
+        load_d[i].wait()
+        if i + 1 < TILES:
+            load_d[i + 1].start()
+            load_g[i + 1].start()
+        rows = pl.ds(i * tall, tall)
+        for at in range(WIDTH // 128):
+            dec_stage[i, pl.ds(at, tall, stride=WIDTH // 128), :] = d[rows, pl.ds(at * 128, 128)].astype(F32)
+        lines = tall * (WIDTH // 128)
+        write(dec_stage.at[i], dec_out.at[pl.ds(i * lines, lines)], wsem.at[i])
+        if i == 0:
+            load_p.wait()
+        load_g[i].wait()
+        rows = pl.ds(i * wide, wide)
+        enc_stage[i] = rows_dot(g[:, rows], p[...])
+        write(enc_stage.at[i], enc_out.at[rows], esem.at[i])
+    for copy in writes:
+        copy.wait()
+
+
+def finish(g, p, d, low_sum, plow_sum):
+    any_spec = pl.BlockSpec(memory_space=pl.ANY)
+    vmem = pl.BlockSpec(memory_space=pltpu.VMEM)
+    V = pltpu.VMEM
+    lines = LATS * (WIDTH // 128)
     return pl.pallas_call(
-        enc_kernel,
-        grid=(n,),
-        out_shape=[jax.ShapeDtypeStruct((WIDTH, LATS), F32), jax.ShapeDtypeStruct((8, LATS), F32)],
-        in_specs=[
-            pl.BlockSpec((TOKENS, w), lambda i: (0, i)),
-            pl.BlockSpec((TOKENS, LATS), lambda i: (0, 0)),
+        finish_kernel,
+        out_shape=[
+            jax.ShapeDtypeStruct((WIDTH, LATS), F32),
+            jax.ShapeDtypeStruct((1, LATS), F32),
+            jax.ShapeDtypeStruct((lines, 128), F32),
+            jax.ShapeDtypeStruct((1, WIDTH), F32),
         ],
-        out_specs=[pl.BlockSpec((w, LATS), lambda i: (i, 0)), pl.BlockSpec((8, LATS), lambda i: (0, 0))],
+        in_specs=[any_spec] * 3 + [vmem] * 2,
+        out_specs=[any_spec, vmem, any_spec, vmem],
+        scratch_shapes=[
+            V((TOKENS, WIDTH), BF16), V((TOKENS, LATS), BF16), V((LATS, WIDTH), BF16),
+            V((TILES, WIDTH // TILES, LATS), F32), V((TILES, lines // TILES, 128), F32),
+            pltpu.SemaphoreType.DMA((1,)),
+            pltpu.SemaphoreType.DMA((TILES,)),
+            pltpu.SemaphoreType.DMA((TILES,)),
+            pltpu.SemaphoreType.DMA((TILES,)),
+            pltpu.SemaphoreType.DMA((TILES,)),
+        ],
         compiler_params=pltpu.CompilerParams(vmem_limit_bytes=56 << 20),
-        name="enc_grads",
-    )(g, p)
-
-
-def dec_kernel(c, r, dec, norm, out, bias_out):
-    sums = rows_dot(c[...], jnp.ones((TOKENS, 128), BF16))
-    factor = (PENALTY * SCALE) * sums / norm[...]
-    for i in range(4):
-        cols = slice(i * 512, (i + 1) * 512)
-        value = rows_dot(c[...], r[:, cols])
-        for j in range(4):
-            at = i * 4 + j
-            part = value[:, j * 128 : (j + 1) * 128]
-            part = part + factor * dec[:, at * 128 : (at + 1) * 128].astype(F32)
-            out[pl.ds(at, part.shape[0], stride=16), :] = part
-
-    @pl.when(pl.program_id(0) == 0)
-    def _():
-        bias_out[...] = jnp.dot(jnp.ones((8, TOKENS), BF16), r[...], preferred_element_type=F32)
-
-
-def dec_grads(c, r, dec, norm):
-    n = 4
-    w = LATS // n
-    return pl.pallas_call(
-        dec_kernel,
-        grid=(n,),
-        out_shape=[jax.ShapeDtypeStruct((LATS * 16, 128), F32), jax.ShapeDtypeStruct((8, WIDTH), F32)],
-        in_specs=[
-            pl.BlockSpec((TOKENS, w), lambda i: (0, i)),
-            pl.BlockSpec((TOKENS, WIDTH), lambda i: (0, 0)),
-            pl.BlockSpec((w, WIDTH), lambda i: (i, 0)),
-            pl.BlockSpec((w, 128), lambda i: (i, 0)),
-        ],
-        out_specs=[pl.BlockSpec((w * 16, 128), lambda i: (i, 0)), pl.BlockSpec((8, WIDTH), lambda i: (0, 0))],
-        compiler_params=pltpu.CompilerParams(vmem_limit_bytes=56 << 20),
-        name="dec_grads",
-    )(c, r, dec, norm)
+        name="finish",
+    )(g, p, d, low_sum, plow_sum)
 
 
 def on_device(acts, enc_weight, enc_bias, dec_weight, dec_bias):
     dec = dec_weight.reshape(LATS, WIDTH)
-    g, c, r, p, norm = exchange(
+    g, p, d, low_sum, plow_sum = exchange(
         acts.reshape(TOKENS // 16, WIDTH), enc_weight.reshape(WIDTH, LATS), enc_bias.reshape(1, LATS), dec, dec_bias
     )
-    g, r = g.reshape(TOKENS, WIDTH), r.reshape(TOKENS, WIDTH)
-    c, p = c.reshape(TOKENS, LATS), p.reshape(TOKENS, LATS)
-    dec_grad, dec_bias_grad = dec_grads(c, r, dec, norm)
-    enc_grad, enc_bias_grad = enc_grads(g, p)
+    g, p = g.reshape(TOKENS, WIDTH), p.reshape(TOKENS, LATS)
+    enc_grad, enc_bias_grad, dec_grad, dec_bias_grad = finish(g, p, d, low_sum, plow_sum)
     return (
         enc_grad.reshape(1, WIDTH, LATS),
-        enc_bias_grad[0],
+        enc_bias_grad.reshape(LATS),
         dec_grad.reshape(LATS, 1, WIDTH),
-        dec_bias_grad[0:1],
+        dec_bias_grad,
     )
 
 

time: 154 us -> 141 us (0.916)
  Pallas kernels: 148 us -> 138 us
  local copies, waits for them, and re-layouts: 2.79 us -> 0 us
    pallas_call x2 -> x1, Pallas kernels: 23.9 us -> 13.7 us  [finish(): pl.pallas_call(finish_kernel, out_shape=[jax.ShapeDtypeStruct((WIDTH, LAT...]
    slice x2 -> x0, local copies, waits for them, and re-layouts: 2.79 us -> none  [the longest x1 1.44 us: on_device(): dec_bias_grad[0:1]]
where the time goes in v3:
time: 141 us; the launch traced here: 139 us
  Pallas kernels  138 us (98%)
    pallas_call x1, Pallas kernels, exchange(): pl.pallas_call(step_kernel, out_shape=[jax.ShapeDtypeStruct(by_latent, BF...  125 us
    pallas_call x1, Pallas kernels, finish(): pl.pallas_call(finish_kernel, out_shape=[jax.ShapeDtypeStruct((WIDTH, LAT...  13.7 us

profile of v3, /device:TPU:96, one launch (start us, length us, event | category | flops | bytes accessed | tf_op | source)
XLA Modules:
  0.0 138.8 jit_solution(8889400063227796368)
XLA Ops:
  0.6 124.5 %exchange.1 = (bf16[8,2,4,16,2048]{4,3,2,1,0:T(8,128)(2,1)}, bf16[8,4,2,16,1024]{4,3,2,1,0:T(8,128)(2,1)}, bf16[1024,2048]{1,0:T(8,128)(2,1)}, f32[8,2048]{1,0:T(8,128)}, f32[8,1024]{1,0:T(8,128)}) custom-call(bf16[64,2048]{1,0:T(8,128)(2,1)} %bitcast.13, bf16[2048,1024]{1,0:T(8,128)(2,1)} %bitcast.9, f32[1,1024]{1,0:T(1,128)} %bitcast.14, ...), custom_call_target="tpu_custom_call" | custom-call | tf_op jit(solution)/shard_map/exchange/pallas_call | solution.py:428
  125.2 13.7 %finish.1 = (f32[2048,1024]{1,0:T(8,128)}, f32[1,1024]{1,0:T(1,128)}, f32[16384,128]{1,0:T(8,128)}, f32[1,2048]{1,0:T(1,128)}) custom-call(bf16[1024,2048]{1,0:T(8,128)(2,1)} %bitcast.11, bf16[1024,1024]{1,0:T(8,128)(2,1)} %bitcast.12, bf16[1024,2048]{1,0:T(8,128)(2,1)} %get-tuple-element.15.d_hbm, f32[8,2048]{1,0:T(8,128)} %get-tuple-element.16.low_sum, ...), custom_call_target="tpu_custom_call" | custom-call | tf_op jit(solution)/shard_map/finish/pallas_call | solution.py:515

commit v4 on v3

--- a/solution.py
+++ b/solution.py
@@ -25,6 +25,7 @@
 TILE = 512
 
 SEMS = 25
+FAR_FIRST = (2, 1, 3)
 
 HOPS = (1.0,) * 17
 STARTS = tuple(sum(HOPS[:m]) for m in range(len(HOPS) + 1))
@@ -121,11 +122,13 @@
     mine = pl.ds(aligned(zh * PART, PART), PART)
     theirs = pl.ds(aligned((1 - zh) * PART, PART), PART)
 
-    def sum_send(sem, k, bufs):
+    def sum_send(sem, k, bufs, part):
         send, ya, zb = bufs["send"], bufs["ya"], bufs["zb"]
-        push(sem + 1, k, send.at[k, :, 1 - zl, :, right], zb.at[k], zldev)
-        for d in (1, 2, 3):
-            push(sem, k, send.at[k, (y + d) % 4, :, :, left], ya.at[k, d - 1], ydev(d))
+        if part == 0:
+            for d in FAR_FIRST:
+                push(sem, k, send.at[k, (y + d) % 4, :, :, left], ya.at[k, d - 1], ydev(d))
+        else:
+            push(sem + 1, k, send.at[k, :, 1 - zl, :, right], zb.at[k], zldev)
 
     def sum_mid(sem, k, bufs, narrow, wide):
         full, ya, zb, za_send, za, mid, mid_f32, yb, keep = (
@@ -135,7 +138,7 @@
         value = full[k % 2, :, zl, :, right] + wide(zb[k])
         mid_f32[k % 2] = value
         mid[k] = narrow(value)
-        for d in (1, 2, 3):
+        for d in FAR_FIRST:
             push(sem + 3, k, mid.at[k, (y + d) % 4], yb.at[k, d - 1], ydev(d))
         arrived(sem, k, ya.at[k])
 
@@ -161,13 +164,13 @@
     def spread_send(sem, k, buf):
         own, first = buf.at[k, y, zl], buf.at[k, y, zl, :, left]
         push(sem, k, first, first, zldev)
-        for d in (1, 2, 3):
+        for d in FAR_FIRST:
             push(sem + 2, k, own, own, ydev(d))
 
     def spread_mid(sem, k, buf):
         first = buf.at[k, y, 1 - zl, :, left]
         arrived(sem, k, first)
-        for d in (1, 2, 3):
+        for d in FAR_FIRST:
             push(sem + 1, k, first, first, ydev(d))
         arrived(sem + 2, k, buf.at[k, pl.ds(0, 3), 0])
         column = buf.at[k, :, zl, :, right]
@@ -182,14 +185,14 @@
         gath[k + zh, c, x] = acts[pl.ds(aligned(k * 8, 16), 16), :]
         ref = gath.at[k + zh, c, x]
         push(0, k, ref, ref, zhdev)
-        for d in (1, 2, 3):
+        for d in FAR_FIRST:
             push(1, k, ref, ref, xdev(d))
 
     def m1(pair):
         k = 2 * pair
         ref = gath.at[k + 1 - zh, c, x]
         arrived(0, k, ref)
-        for d in (1, 2, 3):
+        for d in FAR_FIRST:
             push(1, k, ref, ref, xdev(d))
 
     def m2(pair):
@@ -205,16 +208,12 @@
         pl.when(k % 2 == 0)(functools.partial(wait_pair, k))
         pltpu.make_async_copy(gath.at[k], g_out.at[k], osem.at[0]).start()
 
-        def tile(n, _):
-            cols = pl.ds(aligned(n * TILE, TILE), TILE)
-            left_rows = gath[k].reshape(ROWS, WIDTH)
-            value = jnp.dot(left_rows, enc[:, cols], preferred_element_type=F32).reshape(4, 2, 16, TILE)
+        for part, cols in enumerate((left, right)):
+            rows = gath[k].reshape(ROWS, WIDTH)
+            value = jnp.dot(rows, enc[:, cols], preferred_element_type=F32).reshape(4, 2, 16, HALF)
             sums1["full"][k % 2, :, :, :, cols] = value
             sums1["send"][k, :, :, :, cols] = pack(value)
-            return 0
-
-        lax.fori_loop(0, LATS // TILE, tile, 0)
-        sum_send(3, k, sums1)
+            sum_send(3, k, sums1, part)
 
     def m4(k):
         sum_mid(3, k, sums1, pack, unpack)
@@ -255,7 +254,7 @@
 
     def m8(k):
         arrived(11, k, crecv.at[k])
-        for d in (1, 2, 3):
+        for d in FAR_FIRST:
             to = (x + d) % 4
             xsend[k, d - 1] = (full3[k % 2, c, to] + crecv[k, to].astype(F32)).astype(BF16)
             push(12, k, xsend.at[k, d - 1], xrecv.at[k, d - 1], xdev(d))
@@ -280,13 +279,13 @@
         low[k, c, x, :, mine] = ((recon - flat) * SCALE).astype(BF16)
         ref = low.at[k, c, x, :, mine]
         push(14, k, ref, ref, zhdev)
-        for d in (1, 2, 3):
+        for d in FAR_FIRST:
             push(15, k, ref, ref, xdev(d))
 
     def m11(k):
         ref = low.at[k, c, x, :, theirs]
         arrived(14, k, ref)
-        for d in (1, 2, 3):
+        for d in FAR_FIRST:
             push(15, k, ref, ref, xdev(d))
 
     def m12(k):
@@ -297,17 +296,13 @@
     def m13(k):
         arrived(16, k, low.at[k, 1 - c])
 
-        def tile(n, _):
-            cols = pl.ds(aligned(n * TILE, TILE), TILE)
+        for part, cols in enumerate((left, right)):
             rows = low[k].reshape(ROWS, WIDTH)
             value = jnp.dot(rows, dec_t[:, cols], preferred_element_type=F32)
-            value = (value + (PENALTY * SCALE) * norm_row[0:1, cols]).reshape(4, 2, 16, TILE)
+            value = (value + (PENALTY * SCALE) * norm_row[0:1, cols]).reshape(4, 2, 16, HALF)
             sums2["full"][k % 2, :, :, :, cols] = value
             sums2["send"][k, :, :, :, cols] = value.astype(BF16)
-            return 0
-
-        lax.fori_loop(0, LATS // TILE, tile, 0)
-        sum_send(17, k, sums2)
+            sum_send(17, k, sums2, part)
         add_rows(low_sum, k, low[k].reshape(ROWS, WIDTH))
 
     def m14(k):

time: 141 us -> 137 us (0.972)
  Pallas kernels: 138 us -> 134 us
    pallas_call x1, Pallas kernels: 125 us -> 120 us  [exchange(): pl.pallas_call(step_kernel, out_shape=[jax.ShapeDtypeStruct(by_latent, BF...]
where the time goes in v4:
time: 137 us; the launch traced here: 134 us
  Pallas kernels  134 us (98%)
    pallas_call x1, Pallas kernels, exchange(): pl.pallas_call(step_kernel, out_shape=[jax.ShapeDtypeStruct(by_latent, BF...  120 us
    pallas_call x1, Pallas kernels, finish(): pl.pallas_call(finish_kernel, out_shape=[jax.ShapeDtypeStruct((WIDTH, LAT...  13.7 us

profile of v4, /device:TPU:96, one launch (start us, length us, event | category | flops | bytes accessed | tf_op | source)
XLA Modules:
  0.0 134.4 jit_solution(6059987564936843762)
XLA Ops:
  0.6 120.1 %exchange.1 = (bf16[8,2,4,16,2048]{4,3,2,1,0:T(8,128)(2,1)}, bf16[8,4,2,16,1024]{4,3,2,1,0:T(8,128)(2,1)}, bf16[1024,2048]{1,0:T(8,128)(2,1)}, f32[8,2048]{1,0:T(8,128)}, f32[8,1024]{1,0:T(8,128)}) custom-call(bf16[64,2048]{1,0:T(8,128)(2,1)} %bitcast.13, bf16[2048,1024]{1,0:T(8,128)(2,1)} %bitcast.9, f32[1,1024]{1,0:T(1,128)} %bitcast.14, ...), custom_call_target="tpu_custom_call" | custom-call | tf_op jit(solution)/shard_map/exchange/pallas_call | solution.py:423
  120.8 13.7 %finish.1 = (f32[2048,1024]{1,0:T(8,128)}, f32[1,1024]{1,0:T(1,128)}, f32[16384,128]{1,0:T(8,128)}, f32[1,2048]{1,0:T(1,128)}) custom-call(bf16[1024,2048]{1,0:T(8,128)(2,1)} %bitcast.11, bf16[1024,1024]{1,0:T(8,128)(2,1)} %bitcast.12, bf16[1024,2048]{1,0:T(8,128)(2,1)} %get-tuple-element.15.d_hbm, f32[8,2048]{1,0:T(8,128)} %get-tuple-element.16.low_sum, ...), custom_call_target="tpu_custom_call" | custom-call | tf_op jit(solution)/shard_map/finish/pallas_call | solution.py:510

commit v5 on v4

--- a/solution.py
+++ b/solution.py
@@ -19,12 +19,14 @@
 LATS = 1024
 HALF = LATS // 2
 PART = WIDTH // 2
+FIRST = 768
+REST = PART - FIRST
 CHUNKS = 8
 ROWS = TOKENS // CHUNKS
 SCALE = 1.0 / math.sqrt(TOKENS)
 TILE = 512
 
-SEMS = 25
+SEMS = 27
 FAR_FIRST = (2, 1, 3)
 
 HOPS = (1.0,) * 17
@@ -71,11 +73,11 @@
 
 
 def step_kernel(
-    acts, enc_hbm, enc_bias, dec_hbm, dec_bias,
+    acts_hbm, enc_hbm, enc_bias, dec_hbm, dec_bias,
     g_out, p_out, d_out, low_sum, plow_sum,
-    enc, dec, dec_t, gath, codes, low, plow,
+    acts, enc, dec, dec_t, gath, codes, low, plow,
     sums1, sums2, active,
-    full3, send3, crecv, xsend, xrecv, zsend3, zrecv3, keep3, norm_row, norm_wide, factor, code_sum, products,
+    full3, send3, crecv, xsend, xrecv, zsend3, zrecv3, zb_send, zb_recv, xb_send, xb_recv, keep3, keep_rest, norm_row, norm_wide, factor, code_sum, spread, products,
     ssem, rsem, lsem, osem,
 ):
     a = lax.axis_index("layer")
@@ -94,15 +96,17 @@
     zhdev = (a, x * 4 + (1 - zh) * 2 + c)
     cdev = (a, x * 4 + zh * 2 + 1 - c)
 
-    load_enc = pltpu.make_async_copy(enc_hbm, enc, lsem.at[0])
-    load_dec = pltpu.make_async_copy(dec_hbm, dec, lsem.at[1])
-    load_enc.start()
-    load_dec.start()
-
     barrier = pltpu.get_barrier_semaphore()
     peers = [zldev, zhdev, cdev] + [ydev(d) for d in (1, 2, 3)] + [xdev(d) for d in (1, 2, 3)]
     for peer in peers:
         pl.semaphore_signal(barrier, inc=1, device_id=peer, device_id_type=MESH)
+    load_acts = pltpu.make_async_copy(acts_hbm, acts, lsem.at[2])
+    load_enc = pltpu.make_async_copy(enc_hbm, enc, lsem.at[0])
+    load_dec = pltpu.make_async_copy(dec_hbm, dec, lsem.at[1])
+    load_acts.start()
+    load_enc.start()
+    load_dec.start()
+    load_acts.wait()
     pl.semaphore_wait(barrier, len(peers))
 
     def push(sem, k, src, dst, device):
@@ -252,31 +256,56 @@
             total = jnp.sum(code_sum[...], axis=0, keepdims=True) * (PENALTY * SCALE)
             factor[...] = jnp.broadcast_to(total, (128, LATS)).T / norm_wide[...]
 
+    def pair_sum(k, block, cols):
+        return full3[k % 2, c, block, :, cols] + crecv[k, block, :, cols].astype(F32)
+
+    def first_of(half):
+        return pl.ds(aligned(half * PART, PART), FIRST)
+
+    def rest_of(half):
+        return pl.ds(aligned(half * PART + FIRST, REST), REST)
+
     def m8(k):
         arrived(11, k, crecv.at[k])
         for d in FAR_FIRST:
             to = (x + d) % 4
-            xsend[k, d - 1] = (full3[k % 2, c, to] + crecv[k, to].astype(F32)).astype(BF16)
+            for half in range(2):
+                xsend[k, d - 1, :, pl.ds(half * FIRST, FIRST)] = pair_sum(k, to, first_of(half)).astype(BF16)
             push(12, k, xsend.at[k, d - 1], xrecv.at[k, d - 1], xdev(d))
+        for block in range(4):
+            zb_send[k, block] = pair_sum(k, block, rest_of(1 - zh)).astype(BF16)
+        push(25, k, zb_send.at[k], zb_recv.at[k], zhdev)
 
     def m9(k):
+        arrived(25, k, zb_recv.at[k])
+        for d in FAR_FIRST:
+            to = (x + d) % 4
+            value = pair_sum(k, to, rest_of(zh)) + zb_recv[k, to].astype(F32)
+            xb_send[k, d - 1] = value.astype(BF16)
+            push(26, k, xb_send.at[k, d - 1], xb_recv.at[k, d - 1], xdev(d))
+        keep_rest[k % 2] = pair_sum(k, x, rest_of(zh)) + zb_recv[k, x].astype(F32)
         arrived(12, k, xrecv.at[k])
 
-        def total(cols):
-            value = full3[k % 2, c, x, :, cols] + crecv[k, x, :, cols].astype(F32)
+        def total(half):
+            value = pair_sum(k, x, first_of(half))
             for d in range(3):
-                value = value + xrecv[k, d, :, cols].astype(F32)
+                value = value + xrecv[k, d, :, pl.ds(aligned(half * FIRST, FIRST), FIRST)].astype(F32)
             return value
 
-        zsend3[k] = total(theirs).astype(BF16)
+        zsend3[k] = total(1 - zh).astype(BF16)
         push(13, k, zsend3.at[k], zrecv3.at[k], zhdev)
-        keep3[k % 2] = total(mine)
+        keep3[k % 2] = total(zh)
 
     def m10(k):
+        arrived(26, k, xb_recv.at[k])
+        rest = keep_rest[k % 2]
+        for d in range(3):
+            rest = rest + xb_recv[k, d].astype(F32)
         arrived(13, k, zrecv3.at[k])
-        recon = keep3[k % 2] + zrecv3[k].astype(F32) + dec_bias[:, mine]
-        flat = gath[k, c, x, :, mine].astype(F32)
-        low[k, c, x, :, mine] = ((recon - flat) * SCALE).astype(BF16)
+        first = keep3[k % 2] + zrecv3[k].astype(F32)
+        for recon, cols in ((first, first_of(zh)), (rest, rest_of(zh))):
+            flat = gath[k, c, x, :, cols].astype(F32)
+            low[k, c, x, :, cols] = ((recon + dec_bias[:, cols] - flat) * SCALE).astype(BF16)
         ref = low.at[k, c, x, :, mine]
         push(14, k, ref, ref, zhdev)
         for d in FAR_FIRST:
@@ -331,15 +360,26 @@
         norm_row[:, rows] = wide.T[0:8, :]
         dec_t[:, rows] = block.T
 
+    lines = LATS * (WIDTH // 128) // 4
+
+    def product_out(n):
+        part = pl.ds(aligned(n * lines, lines), lines)
+        return part, pltpu.make_async_copy(products.at[part], d_out.at[part], osem.at[2])
+
     def decoder_product(n):
         rows = pl.ds(aligned(n * (LATS // 4), LATS // 4), LATS // 4)
         left_side = codes[:, :, :, :, rows].reshape(TOKENS, LATS // 4)
-        for half in (lower, upper):
-            right_side = low[:, :, :, :, half].reshape(TOKENS, PART)
+        for half in range(2):
+            right_side = low[:, :, :, :, pl.ds(half * PART, PART)].reshape(TOKENS, PART)
             value = rows_dot(left_side, right_side)
-            penalty = jnp.tile(factor[rows, :], (1, PART // 128)) * dec[rows, half].astype(F32)
-            products[rows, half] = (value + penalty).astype(BF16)
-        pltpu.make_async_copy(products.at[rows], d_out.at[rows], osem.at[2]).start()
+            for j in range(PART // 128):
+                at = half * (PART // 128) + j
+                part = value[:, j * 128 : (j + 1) * 128]
+                part = part + factor[rows, :] * dec[rows, pl.ds(at * 128, 128)].astype(F32)
+                spread[pl.ds(at, LATS // 4, stride=WIDTH // 128), :] = part
+        part, out = product_out(n)
+        products[part, :] = spread[...].astype(BF16)
+        out.start()
 
     stages = [m0, m1, m2, m3, m4, m5, m6, m7, m8, m9, m10, m11, m12, m13, m14, m15, m16, m17]
 
@@ -387,7 +427,9 @@
         gone(11, k, crecv.at[k])
         gone(12, k, xsend.at[k])
         gone(13, k, zsend3.at[k])
-        gone(14, k, zsend3.at[k])
+        gone(14, k, low.at[k, 0, 0, :, lower])
+        gone(25, k, zb_send.at[k])
+        gone(26, k, xb_send.at[k])
         gone(15, k, low.at[k, 0, pl.ds(0, 3)])
         gone(16, k, low.at[k, 0])
         return 0
@@ -425,24 +467,28 @@
         out_shape=[
             jax.ShapeDtypeStruct(by_latent, BF16),
             jax.ShapeDtypeStruct(by_layer, BF16),
-            jax.ShapeDtypeStruct((LATS, WIDTH), BF16),
+            jax.ShapeDtypeStruct((LATS * (WIDTH // 128), 128), BF16),
             jax.ShapeDtypeStruct((8, WIDTH), F32),
             jax.ShapeDtypeStruct((8, LATS), F32),
         ],
-        in_specs=[vmem, any_spec, vmem, any_spec, vmem],
+        in_specs=[any_spec, any_spec, vmem, any_spec, vmem],
         out_specs=[any_spec, any_spec, any_spec, vmem, vmem],
         scratch_shapes=[
+            V((TOKENS // 16, WIDTH), BF16),
             V((WIDTH, LATS), BF16), V((LATS, WIDTH), BF16), V((WIDTH, LATS), BF16),
             V(by_latent, BF16), V(by_layer, BF16), V(by_latent, BF16), V(by_layer, BF16),
             layer_sum(), layer_sum(), V((CHUNKS, 16, LATS), F32),
             V((2, 2, 4, 16, WIDTH), F32), V(by_latent, BF16), V((CHUNKS, 4, 16, WIDTH), BF16),
-            V((CHUNKS, 3, 16, WIDTH), BF16), V((CHUNKS, 3, 16, WIDTH), BF16),
-            V((CHUNKS, 16, PART), BF16), V((CHUNKS, 16, PART), BF16), V((2, 16, PART), F32),
+            V((CHUNKS, 3, 16, 2 * FIRST), BF16), V((CHUNKS, 3, 16, 2 * FIRST), BF16),
+            V((CHUNKS, 16, FIRST), BF16), V((CHUNKS, 16, FIRST), BF16),
+            V((CHUNKS, 4, 16, REST), BF16), V((CHUNKS, 4, 16, REST), BF16),
+            V((CHUNKS, 3, 16, REST), BF16), V((CHUNKS, 3, 16, REST), BF16),
+            V((2, 16, FIRST), F32), V((2, 16, REST), F32),
             V((8, LATS), F32), V((LATS, 128), F32), V((LATS, 128), F32), V((8, LATS), F32),
-            V((LATS, WIDTH), BF16),
+            V((LATS * (WIDTH // 128) // 4, 128), F32), V((LATS * (WIDTH // 128), 128), BF16),
             pltpu.SemaphoreType.DMA((SEMS, CHUNKS)),
             pltpu.SemaphoreType.DMA((SEMS, CHUNKS)),
-            pltpu.SemaphoreType.DMA((2,)),
+            pltpu.SemaphoreType.DMA((3,)),
             pltpu.SemaphoreType.DMA((3,)),
         ],
         compiler_params=pltpu.CompilerParams(
@@ -464,7 +510,7 @@
     enc_out, enc_bias_out, dec_out, dec_bias_out,
     g, p, d, enc_stage, dec_stage, lsem, gsem, dsem, esem, wsem,
 ):
-    wide, tall = WIDTH // TILES, LATS // TILES
+    wide, tall = WIDTH // TILES, LATS * (WIDTH // 128) // TILES
     load_p = pltpu.make_async_copy(p_hbm, p, lsem.at[0])
     load_g, load_d = [], []
     for i in range(TILES):
@@ -488,10 +534,8 @@
             load_d[i + 1].start()
             load_g[i + 1].start()
         rows = pl.ds(i * tall, tall)
-        for at in range(WIDTH // 128):
-            dec_stage[i, pl.ds(at, tall, stride=WIDTH // 128), :] = d[rows, pl.ds(at * 128, 128)].astype(F32)
-        lines = tall * (WIDTH // 128)
-        write(dec_stage.at[i], dec_out.at[pl.ds(i * lines, lines)], wsem.at[i])
+        dec_stage[i] = d[rows, :].astype(F32)
+        write(dec_stage.at[i], dec_out.at[rows], wsem.at[i])
         if i == 0:
             load_p.wait()
         load_g[i].wait()
@@ -518,7 +562,7 @@
         in_specs=[any_spec] * 3 + [vmem] * 2,
         out_specs=[any_spec, vmem, any_spec, vmem],
         scratch_shapes=[
-            V((TOKENS, WIDTH), BF16), V((TOKENS, LATS), BF16), V((LATS, WIDTH), BF16),
+            V((TOKENS, WIDTH), BF16), V((TOKENS, LATS), BF16), V((lines, 128), BF16),
             V((TILES, WIDTH // TILES, LATS), F32), V((TILES, lines // TILES, 128), F32),
             pltpu.SemaphoreType.DMA((1,)),
             pltpu.SemaphoreType.DMA((TILES,)),

time: 137 us -> 134 us (0.978)
  Pallas kernels: 134 us -> 132 us
where the time goes in v5:
time: 134 us; the launch traced here: 133 us
  Pallas kernels  132 us (99%)
    pallas_call x1, Pallas kernels, exchange(): pl.pallas_call(step_kernel, out_shape=[jax.ShapeDtypeStruct(by_latent, BF...  119 us
    pallas_call x1, Pallas kernels, finish(): pl.pallas_call(finish_kernel, out_shape=[jax.ShapeDtypeStruct((WIDTH, LAT...  12.8 us

profile of v5, /device:TPU:96, one launch (start us, length us, event | category | flops | bytes accessed | tf_op | source)
XLA Modules:
  0.0 132.6 jit_solution(16131831568978277469)
XLA Ops:
  0.6 119.2 %exchange.1 = (bf16[8,2,4,16,2048]{4,3,2,1,0:T(8,128)(2,1)}, bf16[8,4,2,16,1024]{4,3,2,1,0:T(8,128)(2,1)}, bf16[16384,128]{1,0:T(8,128)(2,1)}, f32[8,2048]{1,0:T(8,128)}, f32[8,1024]{1,0:T(8,128)}) custom-call(bf16[64,2048]{1,0:T(8,128)(2,1)} %bitcast.13, bf16[2048,1024]{1,0:T(8,128)(2,1)} %bitcast.9, f32[1,1024]{1,0:T(1,128)} %bitcast.14, ...), custom_call_target="tpu_custom_call" | custom-call | tf_op jit(solution)/shard_map/exchange/pallas_call | solution.py:465
  119.8 12.8 %finish.1 = (f32[2048,1024]{1,0:T(8,128)}, f32[1,1024]{1,0:T(1,128)}, f32[16384,128]{1,0:T(8,128)}, f32[1,2048]{1,0:T(1,128)}) custom-call(bf16[1024,2048]{1,0:T(8,128)(2,1)} %bitcast.11, bf16[1024,1024]{1,0:T(8,128)(2,1)} %bitcast.12, bf16[16384,128]{1,0:T(8,128)(2,1)} %get-tuple-element.15.d_hbm, f32[8,2048]{1,0:T(8,128)} %get-tuple-element.16.low_sum, ...), custom_call_target="tpu_custom_call" | custom-call | tf_op jit(solution)/shard_map/finish/pallas_call | solution.py:554

commit v6 on v5

--- a/solution.py
+++ b/solution.py
@@ -64,12 +64,13 @@
     return jnp.where(coded < 0.0, -size, size)
 
 
-def plain(value):
-    return value.astype(BF16)
-
-
-def widen(value):
-    return value.astype(F32)
+def pack_square(value):
+    return (value * jnp.abs(value)).astype(BF16)
+
+
+def unpack_square(coded):
+    coded = coded.astype(F32)
+    return coded * lax.rsqrt(jnp.maximum(jnp.abs(coded), FLOOR))
 
 
 def step_kernel(
@@ -330,15 +331,15 @@
             value = jnp.dot(rows, dec_t[:, cols], preferred_element_type=F32)
             value = (value + (PENALTY * SCALE) * norm_row[0:1, cols]).reshape(4, 2, 16, HALF)
             sums2["full"][k % 2, :, :, :, cols] = value
-            sums2["send"][k, :, :, :, cols] = value.astype(BF16)
+            sums2["send"][k, :, :, :, cols] = pack_square(value)
             sum_send(17, k, sums2, part)
         add_rows(low_sum, k, low[k].reshape(ROWS, WIDTH))
 
     def m14(k):
-        sum_mid(17, k, sums2, plain, widen)
+        sum_mid(17, k, sums2, pack_square, unpack_square)
 
     def m15(k):
-        for value, cols in zip(sum_end(17, k, sums2, widen), (left, right)):
+        for value, cols in zip(sum_end(17, k, sums2, unpack_square), (left, right)):
             plow[k, y, zl, :, cols] = (value * (2.0 * active[k, :, cols])).astype(BF16)
         spread_send(21, k, plow)
 

time: 134 us -> 135 us (level); the launches traced: 133 us -> 132 us
  no operation moved by 1% of the time
where the time goes in v6:
time: 135 us; the launch traced here: 132 us
  Pallas kernels  131 us (97%)
    pallas_call x1, Pallas kernels, exchange(): pl.pallas_call(step_kernel, out_shape=[jax.ShapeDtypeStruct(by_latent, BF...  119 us
    pallas_call x1, Pallas kernels, finish(): pl.pallas_call(finish_kernel, out_shape=[jax.ShapeDtypeStruct((WIDTH, LAT...  12.8 us

profile of v6, /device:TPU:96, one launch (start us, length us, event | category | flops | bytes accessed | tf_op | source)
XLA Modules:
  0.0 132.0 jit_solution(17779647846474522727)
XLA Ops:
  0.6 118.6 %exchange.1 = (bf16[8,2,4,16,2048]{4,3,2,1,0:T(8,128)(2,1)}, bf16[8,4,2,16,1024]{4,3,2,1,0:T(8,128)(2,1)}, bf16[16384,128]{1,0:T(8,128)(2,1)}, f32[8,2048]{1,0:T(8,128)}, f32[8,1024]{1,0:T(8,128)}) custom-call(bf16[64,2048]{1,0:T(8,128)(2,1)} %bitcast.13, bf16[2048,1024]{1,0:T(8,128)(2,1)} %bitcast.9, f32[1,1024]{1,0:T(1,128)} %bitcast.14, ...), custom_call_target="tpu_custom_call" | custom-call | tf_op jit(solution)/shard_map/exchange/pallas_call | solution.py:466
  119.2 12.8 %finish.1 = (f32[2048,1024]{1,0:T(8,128)}, f32[1,1024]{1,0:T(1,128)}, f32[16384,128]{1,0:T(8,128)}, f32[1,2048]{1,0:T(1,128)}) custom-call(bf16[1024,2048]{1,0:T(8,128)(2,1)} %bitcast.11, bf16[1024,1024]{1,0:T(8,128)(2,1)} %bitcast.12, bf16[16384,128]{1,0:T(8,128)(2,1)} %get-tuple-element.15.d_hbm, f32[8,2048]{1,0:T(8,128)} %get-tuple-element.16.low_sum, ...), custom_call_target="tpu_custom_call" | custom-call | tf_op jit(solution)/shard_map/finish/pallas_call | solution.py:555
